TPU v7x, 32 devices: a whole 2x2x4 slice. The times are simulated.
32 devices in a mesh: dp: 8 (over z, y), head: 4 (over x, core).
Axes of the slice: x: 2, y: 2, z: 4, core: 2. Of those that a mesh axis runs over, the one named last changes fastest.
Arguments:
- tokens: bfloat16 [8192, 768], P(('dp', 'head'))
- w_qkv: bfloat16 [768, 2304], replicated
- w_out: bfloat16 [768, 768], replicated, may hold values from -0.21875 to 0.21875
- w_up: bfloat16 [768, 3072], replicated, may hold values from -0.21875 to 0.21875
- w_down: bfloat16 [3072, 768], replicated, may hold values from -0.109375 to 0.109375
- norm_gains: float32 [2, 768], replicated, may hold values from 0.5 to 1.5
- norm_shifts: float32 [2, 768], replicated, may hold values from -1.8 to 1.8
- conv_kernels: bfloat16 [12, 33], replicated, may hold values from -1 to 1
- seq_lengths: int32 [8], P('dp'), may hold values from 256 to 1024, as said below
- seg_bounds: int32 [8, 65], P('dp'), may hold values from 0 to 1024, as said below
- out_grad: bfloat16 [8192, 768], P(('dp', 'head')), may hold values from -6 to 6
Outputs:
- output: bfloat16 [8192, 768], P(('dp', 'head'))
- input_grad: bfloat16 [8192, 768], P(('dp', 'head'))
- grad_qkv: float32 [768, 2304], P('dp', 'head')
- grad_out: float32 [768, 768], P('dp', 'head')
- grad_up: float32 [768, 3072], P('dp', 'head')
- grad_down: float32 [3072, 768], P('dp', 'head')
- grad_gains: float32 [2, 768], replicated
- grad_shifts: float32 [2, 768], replicated
- grad_kernels: float32 [12, 33], replicated
Inputs may be any that keep to these rules, and one draw needn't show every extreme that they name: `seq_lengths`: some sequence has 1024 tokens and some has 256. `seg_bounds`: each row starts at 0, ends at the sequence's length and rises, every segment holding at least 2 positions.
All inputs are finite; a program needn't handle non-finite values.
Results may differ from a plain program's by a relative error of at most 0.01.
Values may be sent and summed in bfloat16 or wider, within the bound.
A program may use at most 192 MiB of HBM per device.

v0:
```python
import jax
import jax.numpy as jnp
from jax import lax
from jax.sharding import PartitionSpec as P

NEWTON = 6


highest = lax.Precision.HIGHEST
epsilon = 1e-05


def layer_norm(values, gain, shift):
    center = jnp.mean(values, axis=-1, keepdims=True)
    centred = values - center
    spread_sq = jnp.mean(centred * centred, axis=-1, keepdims=True)
    return centred * lax.rsqrt(spread_sq + epsilon) * gain + shift


def exact_gelu(values):
    return jax.nn.gelu(values, approximate=False)


def shifted_conv(values, kernel):
    slot_len = values.shape[0]
    taps = kernel.shape[0]
    half_width = taps // 2
    padded = jnp.pad(values, ((half_width, half_width), (0, 0)))
    total = jnp.zeros_like(values)
    for offset in range(taps):
        total = total + kernel[offset] * padded[offset : offset + slot_len]
    return total


def nystrom_head(queries, keys, values, kernel, length, bounds):
    slot_len = queries.shape[0]
    mark_count = bounds.shape[0] - 1
    head_dim = queries.shape[1]
    places = jnp.arange(slot_len, dtype=jnp.int32)
    valid = places < length
    weight_mask = valid.astype(jnp.float32)[:, None]
    scaling = head_dim ** (-0.25)
    queries = queries * weight_mask * scaling
    keys = keys * weight_mask * scaling
    values = values * weight_mask
    member = ((places[None, :] >= bounds[:-1, None]) & (places[None, :] < bounds[1:, None])).astype(
        jnp.float32
    )
    counts = (bounds[1:] - bounds[:-1]).astype(jnp.float32)[:, None]
    query_marks = jnp.dot(member, queries, precision=highest) / counts
    key_marks = jnp.dot(member, keys, precision=highest) / counts
    first = jax.nn.softmax(jnp.dot(queries, key_marks.T, precision=highest), axis=-1)
    middle = jax.nn.softmax(jnp.dot(query_marks, key_marks.T, precision=highest), axis=-1)
    third_scores = jnp.dot(query_marks, keys.T, precision=highest)
    third = jax.nn.softmax(jnp.where(valid[None, :], third_scores, -1000000000.0), axis=-1)
    inverse = middle.T / (jnp.max(jnp.sum(middle, axis=0)) * jnp.max(jnp.sum(middle, axis=1)))
    identity = jnp.eye(mark_count, dtype=jnp.float32)
    for _ in range(NEWTON):
        product = jnp.dot(middle, inverse, precision=highest)
        inner = 7.0 * identity - product
        inner = 15.0 * identity - jnp.dot(product, inner, precision=highest)
        inner = 13.0 * identity - jnp.dot(product, inner, precision=highest)
        inverse = 0.25 * jnp.dot(inverse, inner, precision=highest)
    summary = jnp.dot(third, values, precision=highest)
    mixed = jnp.dot(first, jnp.dot(inverse, summary, precision=highest), precision=highest)
    return (mixed + shifted_conv(values, kernel)) * weight_mask


def attend(packed, kernels, lengths, bounds):
    seq_count = lengths.shape[0]
    head_count = kernels.shape[0]
    head_dim = packed.shape[-1] // (3 * head_count)
    grouped = packed.reshape(seq_count, -1, 3, head_count, head_dim)
    over_heads = jax.vmap(nystrom_head, in_axes=(1, 1, 1, 0, None, None), out_axes=1)
    over_seqs = jax.vmap(over_heads, in_axes=(0, 0, 0, None, 0, 0))
    result = over_seqs(
        grouped[:, :, 0], grouped[:, :, 1], grouped[:, :, 2], kernels, lengths, bounds
    )
    return result.reshape(seq_count * grouped.shape[1], head_count * head_dim)


def row_contract(left, right):
    return lax.dot_general(
        left, right, (((0,), (0,)), ((), ())), preferred_element_type=jnp.float32
    )


def to_blocks(matrix, dp_count, quarters):
    total_rows, total_cols = matrix.shape
    shaped = matrix.reshape(dp_count, total_rows // dp_count, quarters, total_cols // quarters)
    return shaped.transpose(0, 2, 1, 3).reshape(total_rows * quarters, total_cols // quarters)


def per_device(
    tokens,
    w_qkv,
    w_out,
    w_up,
    w_down,
    norm_gains,
    norm_shifts,
    conv_kernels,
    seq_lengths,
    seg_bounds,
    out_grad,
):
    quarters = lax.axis_size("head")
    quarter = lax.axis_index("head")
    dp_count = lax.axis_size("dp")
    tok_rows, width = tokens.shape
    seq_count = seq_lengths.shape[0]
    group_rows = tok_rows * quarters
    slot_len = group_rows // seq_count
    head_count, kernel_len = conv_kernels.shape
    local_heads = head_count // quarters
    head_width = w_qkv.shape[1] // (3 * quarters)
    places = quarter * tok_rows + jnp.arange(tok_rows, dtype=jnp.int32)
    owners = places // slot_len
    within = places % slot_len
    limits = jnp.sum(
        jnp.where(
            owners[:, None] == jnp.arange(seq_count, dtype=jnp.int32)[None, :],
            seq_lengths[None, :],
            0,
        ),
        axis=1,
    )
    live = (within < limits).astype(jnp.float32)[:, None]
    local_kernels = lax.dynamic_slice_in_dim(
        conv_kernels.astype(jnp.float32), quarter * local_heads, local_heads, 0
    )
    projected = jnp.dot(tokens, w_qkv, preferred_element_type=jnp.float32).astype(jnp.bfloat16)
    packed = lax.all_to_all(
        projected.reshape(tok_rows, 3, quarters, head_width),
        "head",
        split_axis=2,
        concat_axis=0,
        tiled=True,
    )
    packed_rows = packed.reshape(group_rows, 3 * head_width)

    def attention_piece(packed_in, kernel_in):
        return attend(packed_in, kernel_in, seq_lengths, seg_bounds)

    attended, attention_back = jax.vjp(
        attention_piece, packed_rows.astype(jnp.float32), local_kernels
    )
    attended_low = attended.astype(jnp.bfloat16)
    heads_rows = lax.all_to_all(
        attended_low.reshape(group_rows, 1, head_width),
        "head",
        split_axis=0,
        concat_axis=1,
        tiled=True,
    ).reshape(tok_rows, width)
    branch = jnp.dot(heads_rows, w_out, preferred_element_type=jnp.float32)
    first_in = tokens.astype(jnp.float32) + branch
    first_norm, first_back = jax.vjp(layer_norm, first_in, norm_gains[0], norm_shifts[0])
    first_low = first_norm.astype(jnp.bfloat16)
    hidden = jnp.dot(first_low, w_up, preferred_element_type=jnp.float32)
    activated, gelu_back = jax.vjp(exact_gelu, hidden)
    act_low = activated.astype(jnp.bfloat16)
    second = jnp.dot(act_low, w_down, preferred_element_type=jnp.float32)
    output, second_back = jax.vjp(layer_norm, first_norm + second, norm_gains[1], norm_shifts[1])
    cotangent = out_grad.astype(jnp.float32) * live
    grad_second_in, grad_gain_two, grad_shift_two = second_back(cotangent)
    grad_second = grad_second_in.astype(jnp.bfloat16)
    grad_down = row_contract(act_low, grad_second)
    grad_act = jnp.dot(grad_second, w_down.T, preferred_element_type=jnp.float32)
    grad_hidden = gelu_back(grad_act)[0].astype(jnp.bfloat16)
    grad_up = row_contract(first_low, grad_hidden)
    grad_first = grad_second_in + jnp.dot(grad_hidden, w_up.T, preferred_element_type=jnp.float32)
    grad_first_in, grad_gain_one, grad_shift_one = first_back(grad_first)
    grad_branch = grad_first_in.astype(jnp.bfloat16)
    grad_wout = row_contract(heads_rows, grad_branch)
    grad_heads = jnp.dot(grad_branch, w_out.T, preferred_element_type=jnp.float32).astype(
        jnp.bfloat16
    )
    heads_grad = lax.all_to_all(
        grad_heads.reshape(tok_rows, quarters, head_width),
        "head",
        split_axis=1,
        concat_axis=0,
        tiled=True,
    ).reshape(group_rows, head_width)
    grad_packed, grad_local_kernels = attention_back(heads_grad.astype(jnp.float32))
    grad_packed_low = grad_packed.astype(jnp.bfloat16).reshape(group_rows, 3, 1, head_width)
    grad_projected = lax.all_to_all(
        grad_packed_low, "head", split_axis=0, concat_axis=2, tiled=True
    ).reshape(tok_rows, 3 * quarters * head_width)
    grad_wqkv = row_contract(tokens, grad_projected)
    input_grad = (
        grad_first_in + jnp.dot(grad_projected, w_qkv.T, preferred_element_type=jnp.float32)
    ).astype(jnp.bfloat16)
    kernel_full = lax.dynamic_update_slice_in_dim(
        jnp.zeros((head_count, kernel_len), jnp.float32),
        grad_local_kernels,
        quarter * local_heads,
        0,
    )
    small_sums = lax.psum(
        (
            jnp.stack([grad_gain_one, grad_gain_two]),
            jnp.stack([grad_shift_one, grad_shift_two]),
            kernel_full,
        ),
        ("dp", "head"),
    )
    blocked_qkv = to_blocks(grad_wqkv, dp_count, quarters)
    blocked_out = to_blocks(grad_wout, dp_count, quarters)
    blocked_up = to_blocks(grad_up, dp_count, quarters)
    blocked_down = to_blocks(grad_down, dp_count, quarters)
    weight_sums = (
        lax.psum_scatter(blocked_qkv, ("dp", "head"), scatter_dimension=0, tiled=True),
        lax.psum_scatter(blocked_out, ("dp", "head"), scatter_dimension=0, tiled=True),
        lax.psum_scatter(blocked_up, ("dp", "head"), scatter_dimension=0, tiled=True),
        lax.psum_scatter(blocked_down, ("dp", "head"), scatter_dimension=0, tiled=True),
    )
    return (
        output.astype(jnp.bfloat16),
        input_grad,
        weight_sums[0],
        weight_sums[1],
        weight_sums[2],
        weight_sums[3],
        small_sums[0],
        small_sums[1],
        small_sums[2],
    )


def solution(mesh):
    placed = (
        P(("dp", "head"), None),
        P(),
        P(),
        P(),
        P(),
        P(),
        P(),
        P(),
        P("dp"),
        P("dp", None),
        P(("dp", "head"), None),
    )
    return jax.shard_map(
        per_device,
        mesh=mesh,
        in_specs=placed,
        out_specs=(
            P(("dp", "head"), None),
            P(("dp", "head"), None),
            P("dp", "head"),
            P("dp", "head"),
            P("dp", "head"),
            P("dp", "head"),
            P(),
            P(),
            P(),
        ),
        check_vma=False,
    )
```

profile of v0, /device:TPU:0, one launch (start us, length us, event | category | flops | bytes accessed | tf_op | source)
XLA Modules:
  0.0 707.8 jit_solution(14396748398735191769)
XLA Ops:
  17.0 4.3 all-to-all-start
  30.4 7.5 %all-to-all-done = bf16[256,3,4,192]{0,3,1,2:T(8,128)(2,1)} async-done(((bf16[256,3,4,192]{0,3,1,2:T(8,128)(2,1)}), bf16[256,3,4,192]{0,3,1,2:T(8,128)(2,1)}, u32[]{:S(2)}, u32[]{:S(2)}) %all-to-all-start) | async-done | bytes 1179680 | tf_op jit(solution)/shard_map/all_to_all | solution.py:133
  81.8 7.9 %fusion.22 = bf16[1,3,1024,64]{2,3,1,0:T(8,128)(2,1)} fusion(f32[3,64,64]{2,1,0:T(8,128)S(1)} %fusion.246, f32[1,3,1024,64]{2,3,1,0:T(8,128)S(1)} %copy-done.7, f32[1024]{0:T(1024)S(1)} %get-tuple-element.162, f32[3]{0:T(128)S(1)} %copy-done.144, f32[3]{0:T(128)S(1)} %copy-done.152, f32[3]{0:T(128)S(1)} %copy-done.154, f32[3]{0:T(128)S(1)} %copy-done.156, ...), kind=kOutput, calls=%fused_computation.48 | convolution fusion | flops 164560896 | bytes 2032012 | tf_op jit(solution)/shard_map/jvp(vmap(vmap()))/dot_general | solution.py:65
  97.2 4.1 all-to-all-start.1
  104.6 4.2 all-to-all-done.1
  122.0 10.1 %multiply_convert_fusion = (bf16[256,3072]{1,0:T(8,128)(2,1)S(1)}, f32[256,3072]{1,0:T(8,128)S(1)}, f32[256,3072]{1,0:T(8,128)S(1)}) fusion(bf16[768,3072]{1,0:T(8,128)(2,1)} %param.14, f32[256,768]{1,0:T(8,128)S(1)} %get-tuple-element.148, f32[768]{0:T(1024)S(1)} %get-tuple-element.53, f32[768]{0:T(1024)S(1)} %get-tuple-element.165, f32[256]{0:T(256)S(1)} %fusion.210, ...), kind=kOutput, calls=%fused_computation.7 | convolution fusion | flops 1260060672 | bytes 13377536 | tf_op jit(solution)/shard_map/dot_general | solution.py:160
  163.7 11.4 %fusion.106 = (f32[3]{0:T(128)}, f32[3]{0:T(128)}, f32[3]{0:T(128)}, f32[3]{0:T(128)}, f32[3]{0:T(128)}, /*index=5*/f32[3]{0:T(128)}, f32[3]{0:T(128)}, f32[3]{0...) fusion(f32[1,3,1024,64]{2,3,1,0:T(8,128)} %fusion.142, ...), kind=kLoop, calls=%fused_computation.276 | loop fusion | flops 6684624 | bytes 2363596 | tf_op jit(solution)/shard_map/transpose(jvp(vmap(vmap())))/reduce_sum | solution.py:31
  209.5 6.8 pad_add_fusion
  224.9 32.3 %all_to_all.48 = bf16[1024,3,1,192]{3,1,2,0:T(4,128)(2,1)} all-to-all(bf16[1024,3,1,192]{3,1,2,0:T(4,128)(2,1)} %copy.411), channel_id=1, replica_groups=mesh['dp'=8,'head'=4] {'head'}, dimensions={0} | all-to-all | bytes 2359296 | tf_op jit(solution)/shard_map/all_to_all | solution.py:188
  257.1 4.4 copy.476
  264.0 5.0 convolution_bitcast_fusion
  269.0 8.0 %copy.414 = f32[768,2304]{1,0:T(8,128)} copy(f32[768,2304]{0,1:T(8,128)} %convolution_bitcast_fusion) | data formatting | bytes 14155776 | tf_op jit(solution)/shard_map/dot_general | solution.py:83
  277.0 10.3 %reshape.1560 = f32[8,96,4,576]{3,2,1,0:T(4,128)} reshape(f32[768,2304]{1,0:T(8,128)} %copy.414) | data formatting | bytes 14155776 | tf_op jit(solution)/shard_map/reshape | solution.py:90
  287.3 7.3 %copy.415 = f32[8,4,96,576]{3,2,1,0:T(8,128)} copy(f32[8,4,96,576]{3,1,2,0:T(4,128)} %bitcast.826) | data formatting | bytes 14155776 | tf_op jit(solution)/shard_map/transpose | solution.py:91
  295.3 6.9 fusion.226
  302.1 12.9 %reshape.1563 = f32[8,96,4,768]{3,2,1,0:T(4,128)} reshape(f32[768,3072]{1,0:T(8,128)} %fusion.226) | data formatting | bytes 18874368 | tf_op jit(solution)/shard_map/reshape | solution.py:90
  315.0 9.3 %copy.417 = f32[8,4,96,768]{3,2,1,0:T(8,128)} copy(f32[8,4,96,768]{3,1,2,0:T(4,128)} %bitcast.824) | data formatting | bytes 18874368 | tf_op jit(solution)/shard_map/transpose | solution.py:91
  328.2 5.8 copy.477
  334.1 14.2 %copy.419 = f32[8,4,384,192]{2,1,0,3:T(4,128)} copy(f32[8,4,384,192]{2,0,3,1:T(8,128)} %bitcast.825) | data formatting | bytes 18874368 | tf_op jit(solution)/shard_map/transpose | solution.py:91
  348.3 11.6 %reshape.1566 = f32[12288,192]{0,1:T(8,128)} reshape(f32[8,4,384,192]{2,1,0,3:T(4,128)} %copy.419) | data formatting | bytes 18874368 | tf_op jit(solution)/shard_map/reshape | solution.py:91
  362.0 10.6 %fusion.105 = (f32[3]{0:T(128)S(1)}, f32[3]{0:T(128)S(1)}, f32[3]{0:T(128)S(1)}, f32[3]{0:T(128)S(1)}, f32[3]{0:T(128)S(1)}, /*index=5*/f32[3]{0:T(128)S(1)}, f3...) fusion(f32[1,3,1024,64]{2,3,1,0:T(8,128)} %fusion.142, ...), kind=kLoop, calls=%fused_computation.275 | loop fusion | flops 6881229 | bytes 1577164 | tf_op jit(solution)/shard_map/transpose(jvp(vmap(vmap())))/reduce_sum | solution.py:31
  376.2 41.2 %all-reduce.70 = (f32[2,768]{1,0:T(2,128)}, f32[2,768]{1,0:T(2,128)}, f32[12,33]{1,0:T(8,128)}) all-reduce(f32[2,768]{1,0:T(2,128)S(1)} %pad_maximum_fusion, f32[2,768]{1,0:T(2,128)} %pad_maximum_fusion.1, f32[12,33]{1,0:T(8,128)S(1)} %dynamic_update_slice.3), channel_id=1, replica_groups=mesh['dp'=8,'head'=4] {'dp','head'}, use_global_device_ids=true, to_apply=%region_30.31 | all-reduce | flops 3468 | bytes 27744 | tf_op jit(solution)/shard_map/psum | solution.py:201
  420.7 139.3 %reduce-scatter.9.cloned.1.call-done = f32[96,768]{1,0:T(8,128)} async-done(((f32[3072,768]{1,0:T(8,128)}), f32[96,768]{1,0:T(8,128)}) %reduce-scatter.9.cloned.1.call-update) | async-done | bytes 294928 | tf_op jit(solution)/shard_map/reduce_scatter | solution.py:216
  560.1 141.0 %reduce-scatter.11.cloned.1.call-done = f32[384,192]{0,1:T(8,128)} async-done(((f32[12288,192]{0,1:T(8,128)}), f32[384,192]{0,1:T(8,128)}) %reduce-scatter.11.cloned.1.call-update) | async-done | bytes 294928 | tf_op jit(solution)/shard_map/reduce_scatter | solution.py:217
  (584 shorter events, 173.4 us)
Async XLA Ops:
  17.0 20.8 %all-to-all-start = ((bf16[256,3,4,192]{0,3,1,2:T(8,128)(2,1)}), bf16[256,3,4,192]{0,3,1,2:T(8,128)(2,1)}, u32[]{:S(2)}, u32[]{:S(2)}) async-start(bf16[256,3,4,192]{0,3,1,2:T(8,128)(2,1)} %copy.351), calls=%async_computation | async-start | bytes 2359296 | tf_op jit(solution)/shard_map/all_to_all | solution.py:133
  30.4 17.7 %copy-start.109 = (s32[64]{0:T(128)}, s32[64]{0:T(128)S(1)}, u32[]{:S(2)}) copy-start(s32[64]{0:T(128)S(1)} %get-tuple-element.139) | copy-start | bytes 772
  63.9 10.2 %copy-start.38 = (f32[3,64,64]{1,2,0:T(8,128)S(1)}, f32[3,64,64]{1,2,0:T(8,128)}, u32[]{:S(2)}) copy-start(f32[3,64,64]{1,2,0:T(8,128)} %copy-done.37) | copy-start | bytes 147460
  63.9 10.6 %copy-start.10 = (f32[64,64]{1,0:T(8,128)S(1)}, f32[64,64]{1,0:T(8,128)}, u32[]{:S(2)}) copy-start(f32[64,64]{1,0:T(8,128)} %get-tuple-element.163) | copy-start | bytes 49156
  63.9 10.6 %copy-start.36 = (f32[64,64]{1,0:T(8,128)S(1)}, f32[64,64]{1,0:T(8,128)}, u32[]{:S(2)}) copy-start(f32[64,64]{1,0:T(8,128)} %get-tuple-element.164) | copy-start | bytes 49156
  63.9 10.9 %copy-start.35 = (f32[64,64]{1,0:T(8,128)S(1)}, f32[64,64]{1,0:T(8,128)}, u32[]{:S(2)}) copy-start(f32[64,64]{1,0:T(8,128)} %fusion.207) | copy-start | bytes 49156
  66.5 11.1 %copy-start.13 = (f32[3,64,64]{2,1,0:T(8,128)}, f32[3,64,64]{2,1,0:T(8,128)S(1)}, u32[]{:S(2)}) copy-start(f32[3,64,64]{2,1,0:T(8,128)S(1)} %fusion.224) | copy-start | bytes 147460
  97.2 11.6 %all-to-all-start.1 = ((bf16[4,2,24576]{2,1,0:T(2,128)(2,1)}), bf16[4,2,24576]{2,1,0:T(2,128)(2,1)}, u32[]{:S(2)}, u32[]{:S(2)}) async-start(bf16[4,2,24576]{2,1,0:T(2,128)(2,1)} %reshape.1615), calls=%async_computation.1 | async-start | bytes 786432 | tf_op jit(solution)/shard_map/all_to_all | solution.py:149
  119.7 12.5 %slice-start = ((s8[4718592]{0:T(1024)(128)(4,1)}), s8[4194304]{0:T(1024)(128)(4,1)S(1)}, s32[]{:S(2)}) async-start(s8[4718592]{0:T(1024)(128)(4,1)} %bitcast.874), calls=%async_computation.12 | async-start | bytes 8388608
  121.8 18.8 %copy-start.6 = (f32[256,768]{1,0:T(8,128)}, f32[256,768]{1,0:T(8,128)S(1)}, u32[]{:S(2)}) copy-start(f32[256,768]{1,0:T(8,128)S(1)} %get-tuple-element.148) | copy-start | bytes 2359300
  121.8 18.8 %copy-start.95 = (f32[256]{0:T(256)}, f32[256]{0:T(256)S(1)}, u32[]{:S(2)}) copy-start(f32[256]{0:T(256)S(1)} %broadcast_multiply_fusion.2) | copy-start | bytes 3076
  122.0 18.6 %copy-start.103 = (f32[256]{0:T(256)}, f32[256]{0:T(256)S(1)}, u32[]{:S(2)}) copy-start(f32[256]{0:T(256)S(1)} %fusion.210) | copy-start | bytes 3076
  122.0 10.1 %slice-start.1 = ((s8[4718592]{0:T(1024)(128)(4,1)}), s8[524288]{0:T(1024)(128)(4,1)S(1)}, s32[]{:S(2)}) async-start(s8[4718592]{0:T(1024)(128)(4,1)} %bitcast.874), calls=%async_computation.13 | async-start | bytes 1048576
  147.1 11.6 %all-to-all-start.2 = ((bf16[256,4,192]{0,2,1:T(8,128)(2,1)}), bf16[256,4,192]{0,2,1:T(8,128)(2,1)}, u32[]{:S(2)}, u32[]{:S(2)}) async-start(bf16[256,4,192]{0,2,1:T(8,128)(2,1)} %bitcast.837), calls=%async_computation.2 | async-start | bytes 786432 | tf_op jit(solution)/shard_map/all_to_all | solution.py:179
  151.2 269.5 %reduce-scatter.7.cloned.1.call-start = ((), (), s32[]{:S(2)}) async-start(), calls=%async_computation.9 | async-start | bytes 3244032 | tf_op jit(solution)/shard_map/reduce_scatter | solution.py:215
  154.7 266.0 %reduce-scatter.5.cloned.1.call-start = ((), (), s32[]{:S(2)}) async-start(), calls=%async_computation.8 | async-start | bytes 8110080 | tf_op jit(solution)/shard_map/reduce_scatter | solution.py:214
  163.6 13.8 %copy-start.85 = (f32[3,64,64]{2,1,0:T(8,128)S(1)}, f32[3,64,64]{2,1,0:T(8,128)}, u32[]{:S(2)}) copy-start(f32[3,64,64]{2,1,0:T(8,128)} %fusion.102) | copy-start | bytes 147460
  163.7 14.2 %copy-start.77 = (f32[3,64,64]{2,1,0:T(8,128)S(1)}, f32[3,64,64]{2,1,0:T(8,128)}, u32[]{:S(2)}) copy-start(f32[3,64,64]{2,1,0:T(8,128)} %copy-done.76) | copy-start | bytes 147460
  163.7 14.4 %copy-start.47 = (f32[3,64,64]{2,1,0:T(8,128)S(1)}, f32[3,64,64]{2,1,0:T(8,128)}, u32[]{:S(2)}) copy-start(f32[3,64,64]{2,1,0:T(8,128)} %copy-done.46) | copy-start | bytes 147460
  163.7 14.8 %copy-start.75 = (f32[3,64,64]{2,1,0:T(8,128)S(1)}, f32[3,64,64]{2,1,0:T(8,128)}, u32[]{:S(2)}) copy-start(f32[3,64,64]{2,1,0:T(8,128)} %copy-done.74) | copy-start | bytes 147460
  163.7 15.1 %copy-start.24 = (f32[3,64,64]{2,1,0:T(8,128)S(1)}, f32[3,64,64]{2,1,0:T(8,128)}, u32[]{:S(2)}) copy-start(f32[3,64,64]{2,1,0:T(8,128)} %copy-done.23) | copy-start | bytes 147460
  163.7 15.4 %copy-start.11 = (f32[64,64]{1,0:T(8,128)S(1)}, f32[64,64]{1,0:T(8,128)}, u32[]{:S(2)}) copy-start(f32[64,64]{1,0:T(8,128)} %get-tuple-element.163) | copy-start | bytes 49156
  294.6 265.4 %reduce-scatter.9.cloned.1.call-start = ((), (), s32[]{:S(2)}) async-start(), calls=%async_computation.10 | async-start | bytes 9732096 | tf_op jit(solution)/shard_map/reduce_scatter | solution.py:216
  324.4 376.7 %reduce-scatter.11.cloned.1.call-start = ((), (), s32[]{:S(2)}) async-start(), calls=%async_computation.11 | async-start | bytes 9732096 | tf_op jit(solution)/shard_map/reduce_scatter | solution.py:217
  (179 other events, 755.6 us)
Sparse Core Ops, SparseCore 0:
  158.1 103.9 reduce-scatter.6
  294.8 123.1 reduce-scatter.4
  425.4 134.5 reduce-scatter.8
  566.4 134.6 reduce-scatter.10
where the time goes:
time: 718 us; the launch traced here: 708 us
  waiting for transfers between devices  296 us (41%)
  local copies, waits for them, and re-layouts  138 us (19%)
  matrix products  103 us (14%)
  blocking collectives  73.4 us (10%)
  other arithmetic  66.2 us (9%)
  between operations  18.1 us (3%)
  starting transfers between devices  12.7 us (2%)
    reduce_scatter x1, waiting for transfers between devices, per_device(): lax.psum_scatter(blocked_down, ('dp', 'head'), scatter_dimension=0, tiled...  141 us
    reduce_scatter x1, waiting for transfers between devices, per_device(): lax.psum_scatter(blocked_up, ('dp', 'head'), scatter_dimension=0, tiled=T...  139 us
    psum x1, blocking collectives, per_device(): lax.psum((jnp.stack([grad_gain_one, grad_gain_two]), jnp.stack([grad_shif...  41.2 us
    all_to_all x1, blocking collectives, per_device(): lax.all_to_all(grad_packed_low, 'head', split_axis=0, concat_axis=2, tile...  32.3 us
    transpose x3, local copies, waits for them, and re-layouts, to_blocks(): shaped.transpose(0, 2, 1, 3)  30.9 us
    reshape x2, local copies, waits for them, and re-layouts, to_blocks(): matrix.reshape(dp_count, total_rows // dp_count, quarters, total_cols //...  23.3 us
    reduce_sum x2, other arithmetic, shifted_conv(): total = total + kernel[offset] * padded[offset:offset + slot_len]  21.9 us
    unnamed x396, local copies, waits for them, and re-layouts  21.8 us
  transfers between devices with their start and end apart: 7, of which 5 were waited for; matrix products, arithmetic and copies ran while one was open for 28% of the time, Pallas kernels for 0%

commit v1 on v0

--- a/solution.py
+++ b/solution.py
@@ -1,9 +1,861 @@
+import functools
 import jax
 import jax.numpy as jnp
 from jax import lax
 from jax.sharding import PartitionSpec as P
-
+from jax.experimental import pallas as pl
+from jax.experimental.pallas import tpu as pltpu
+
+MESH = pl.DeviceIdType.MESH
 NEWTON = 6
+F32 = jnp.float32
+BF16 = jnp.bfloat16
+HIGHEST = lax.Precision.HIGHEST
+VMEM = pltpu.VMEM
+
+
+def mm(a, b, ca, cb, precision=None):
+    return lax.dot_general(
+        a, b, (((ca,), (cb,)), ((), ())), precision=precision, preferred_element_type=F32
+    )
+
+
+def halves(value):
+    high = value.astype(BF16)
+    low = (value - high.astype(F32)).astype(BF16)
+    return high, low
+
+
+def left(value):
+    high, low = halves(value)
+    return jnp.concatenate([high, high, low], axis=1)
+
+
+def right(value):
+    high, low = halves(value)
+    return jnp.concatenate([high, low, high], axis=0)
+
+
+def fine(a, b):
+    return mm(left(a), right(b), 1, 0)
+
+
+def eye(size):
+    rows = lax.broadcasted_iota(jnp.int32, (size, size), 0)
+    cols = lax.broadcasted_iota(jnp.int32, (size, size), 1)
+    return (rows == cols).astype(F32)
+
+
+def toeplitz(base):
+    rows = jnp.broadcast_to(base, (128, base.shape[1]))
+    return pltpu.roll(rows, 0, 1, stride=1, stride_axis=0).astype(BF16)
+
+
+def windows(mat):
+    zero = jnp.zeros((mat.shape[0], 128), mat.dtype)
+    wide = jnp.concatenate([zero, mat, zero], axis=1)
+    count = mat.shape[1] // 128
+    return jnp.concatenate([wide[:, 128 * b : 128 * b + 384] for b in range(count)], axis=0)
+
+
+def unwindow(stacked, rows):
+    count = stacked.shape[0] // rows
+    return jnp.concatenate([stacked[rows * b : rows * (b + 1)] for b in range(count)], axis=1)
+
+
+def members(bnd_ref, slot):
+    place = lax.broadcasted_iota(jnp.int32, (bnd_ref.shape[0], slot), 1)
+    inside = (place >= bnd_ref[:, 0:1]) & (place < bnd_ref[:, 1:2])
+    return inside.astype(F32).astype(BF16)
+
+
+def copy_to(src, dst, sems, index, device):
+    return pltpu.make_async_remote_copy(
+        src_ref=src,
+        dst_ref=dst,
+        send_sem=sems.at[0, index],
+        recv_sem=sems.at[1, index],
+        device_id=device,
+        device_id_type=MESH,
+    )
+
+
+def greet(devices):
+    barrier = pltpu.get_barrier_semaphore()
+    for device in devices:
+        pl.semaphore_signal(barrier, inc=1, device_id=device, device_id_type=MESH)
+    pl.semaphore_wait(barrier, len(devices))
+
+
+def forward_kernel(
+    tok_ref, wq_hbm, kb_ref, bnd_ref, cnt_ref, len_ref,
+    heads_ref, all_ref, packed_ref, a1_ref, a3_ref, n1_ref, n2_ref, marks_ref,
+    wfull, wt, att, wsem, sems,
+):
+    dp = lax.axis_index("dp")
+    me = lax.axis_index("head")
+    quarters = lax.axis_size("head")
+    rows, width = tok_ref.shape
+    slot = rows * quarters
+    head_width = att.shape[0]
+    count = bnd_ref.shape[0]
+    dim = 64
+    nh = head_width // dim
+    fetch = pltpu.make_async_copy(wq_hbm, wfull, wsem)
+    fetch.start()
+    peers = [(dp, me ^ k) for k in range(1, quarters)]
+    greet(peers)
+    half = rows // 2
+    near = copy_to(tok_ref, all_ref.at[me], sems, 0, (dp, me ^ 1))
+    near.start()
+    far = []
+    for piece in range(2):
+        part = pl.ds(piece * half, half)
+        sent = copy_to(tok_ref.at[part], all_ref.at[me, part], sems, 1 + piece, (dp, me ^ 2))
+        sent.start()
+        far.append(sent)
+    all_ref[me] = tok_ref[...]
+    fetch.wait()
+    odd = lax.rem(me, 2)
+    for part in range(3):
+        start = pl.multiple_of(part * width + 384 * lax.div(me, 2) + 128 * odd, 128)
+        window = wfull[:, pl.ds(start, 256)]
+        wt[part] = window.T
+    w_own = [wt[part, pl.ds(pl.multiple_of(64 * odd, 64), head_width), :] for part in range(3)]
+    w_own = jnp.concatenate(w_own, axis=0)
+
+    def project(block):
+        lanes = pl.ds(pl.multiple_of(rows * block, rows), rows)
+        packed_ref[:, lanes] = mm(w_own, all_ref[block], 1, 1).astype(BF16)
+
+    project(me)
+    near.wait()
+    project(me ^ 1)
+    onward = []
+    for piece in range(2):
+        part = pl.ds(piece * half, half)
+        far[piece].wait()
+        sent = copy_to(
+            all_ref.at[me ^ 2, part], all_ref.at[me ^ 2, part], sems, 3 + piece, (dp, me ^ 1)
+        )
+        sent.start()
+        onward.append(sent)
+    project(me ^ 2)
+    for sent in onward:
+        sent.wait()
+    project(me ^ 3)
+
+    scale = dim ** (-0.25)
+    member = members(bnd_ref, slot)
+    means = mm(packed_ref[: 2 * head_width], member, 1, 1) * (scale / cnt_ref[...])
+    length = len_ref[...]
+    live = lax.broadcasted_iota(jnp.int32, (1, slot), 1) < length
+    unit = eye(count)
+    state = []
+    for head in range(nh):
+        q_marks_t = means[dim * head : dim * (head + 1)]
+        k_marks_t = means[head_width + dim * head : head_width + dim * (head + 1)]
+        q_marks = q_marks_t.T
+        k_marks = k_marks_t.T
+        marks_ref[head, 0] = q_marks
+        marks_ref[head, 1] = k_marks
+        scores = fine(q_marks, k_marks_t)
+        powers = jnp.exp(scores - jnp.max(scores, axis=1, keepdims=True))
+        middle = powers / jnp.sum(powers, axis=1, keepdims=True)
+        marks_ref[head, 2] = middle
+        cols = jnp.max(jnp.sum(middle, axis=0, keepdims=True), axis=1, keepdims=True)
+        sums = jnp.max(jnp.sum(middle, axis=1, keepdims=True), axis=0, keepdims=True)
+        inverse = middle.T / (cols * sums)
+        product = fine(middle, inverse)
+        state.append((inverse, product))
+
+    def newton(step, carry):
+        out = []
+        for head in range(nh):
+            inverse, product = carry[head]
+            spread = left(product)
+            second = mm(spread, right(product), 1, 0)
+            third = mm(spread, right(second), 1, 0)
+            n1_ref[head, step] = jnp.concatenate([product, second], axis=1)
+            n2_ref[head, step] = jnp.concatenate([third, inverse], axis=1)
+            blend = 0.25 * (13.0 * unit - 15.0 * product + 7.0 * second - third)
+            both = mm(jnp.concatenate([left(inverse), spread], axis=0), right(blend), 1, 0)
+            out.append((both[:count], both[count:]))
+        return tuple(out)
+
+    state = lax.fori_loop(0, NEWTON, newton, tuple(state))
+    for head in range(nh):
+        at = dim * head
+        queries = packed_ref[at : at + dim]
+        keys = packed_ref[head_width + at : head_width + at + dim]
+        values = packed_ref[2 * head_width + at : 2 * head_width + at + dim]
+        values = jnp.where(live, values.astype(F32), 0.0).astype(BF16)
+        k_high, k_low = halves(marks_ref[head, 1] * scale)
+        scores = mm(
+            jnp.concatenate([k_high, k_low], axis=1),
+            jnp.concatenate([queries, queries], axis=0), 1, 0,
+        )
+        powers = jnp.exp(scores - jnp.max(scores, axis=0, keepdims=True))
+        first = powers * (1.0 / jnp.sum(powers, axis=0, keepdims=True))
+        a1_ref[head] = first
+        q_high, q_low = halves(marks_ref[head, 0] * scale)
+        scores = mm(
+            jnp.concatenate([q_high, q_low], axis=1),
+            jnp.concatenate([keys, keys], axis=0), 1, 0,
+        )
+        scores = jnp.where(live, scores, -1e9)
+        powers = jnp.exp(scores - jnp.max(scores, axis=1, keepdims=True))
+        third = powers * (1.0 / jnp.sum(powers, axis=1, keepdims=True))
+        a3_ref[head] = third
+        t_high, t_low = halves(third)
+        summary = mm(jnp.concatenate([t_high, t_low], axis=0), values, 1, 1)
+        summary = summary[:count] + summary[count:]
+        weights = fine(state[head][0], summary)
+        marks_ref[head, 3] = summary
+        marks_ref[head, 4] = weights
+        marks_ref[head, 5] = state[head][0]
+        w_high, w_low = halves(weights.T)
+        f_high, f_low = halves(first)
+        mixed = mm(
+            jnp.concatenate([w_high, w_high, w_low], axis=1),
+            jnp.concatenate([f_high, f_low, f_high], axis=0), 1, 0,
+        )
+        band = toeplitz(kb_ref[head, 0:1])
+        conv = unwindow(mm(windows(values), band, 1, 1), dim)
+        att[at : at + dim] = jnp.where(live, mixed + conv, 0.0).astype(BF16)
+    done = []
+    for k in range(1, quarters):
+        lanes = pl.ds(pl.multiple_of(rows * (me ^ k), rows), rows)
+        sent = copy_to(att.at[:, lanes], heads_ref.at[me], sems, 4 + k, (dp, me ^ k))
+        sent.start()
+        done.append(sent)
+    heads_ref[me] = att[:, pl.ds(pl.multiple_of(rows * me, rows), rows)]
+    for sent in done:
+        sent.wait()
+
+
+def forward_call(tokens, w_qkv, kernel_rows, bounds_two, counts, length, quarters):
+    rows, width = tokens.shape
+    nh = kernel_rows.shape[0]
+    head_width = nh * 64
+    slot = rows * quarters
+    count = bounds_two.shape[0]
+    whole = pl.BlockSpec(memory_space=VMEM)
+    return pl.pallas_call(
+        forward_kernel,
+        out_shape=(
+            jax.ShapeDtypeStruct((quarters, head_width, rows), BF16),
+            jax.ShapeDtypeStruct((quarters, rows, width), BF16),
+            jax.ShapeDtypeStruct((3 * head_width, slot), BF16),
+            jax.ShapeDtypeStruct((nh, count, slot), F32),
+            jax.ShapeDtypeStruct((nh, count, slot), F32),
+            jax.ShapeDtypeStruct((nh, NEWTON, count, 2 * count), F32),
+            jax.ShapeDtypeStruct((nh, NEWTON, count, 2 * count), F32),
+            jax.ShapeDtypeStruct((nh, 6, count, 64), F32),
+        ),
+        in_specs=[whole, pl.BlockSpec(memory_space=pl.ANY), whole, whole, whole, whole],
+        out_specs=[whole] * 8,
+        scratch_shapes=[
+            VMEM(w_qkv.shape, BF16),
+            VMEM((3, 256, width), BF16),
+            VMEM((head_width, slot), BF16),
+            pltpu.SemaphoreType.DMA,
+            pltpu.SemaphoreType.DMA((2, 8)),
+        ],
+        compiler_params=pltpu.CompilerParams(
+            collective_id=0, has_side_effects=True, vmem_limit_bytes=48 * 2**20
+        ),
+    )(tokens, w_qkv, kernel_rows, bounds_two, counts, length)
+
+
+def small_inputs(conv_kernels, seq_lengths, seg_bounds, quarter, local):
+    taps = conv_kernels.shape[1]
+    mine = lax.dynamic_slice_in_dim(conv_kernels.astype(F32), quarter * local, local, 0)
+    both = jnp.stack([mine, mine[:, ::-1]], axis=1)
+    kernel_rows = jnp.pad(both, ((0, 0), (0, 0), (112, 384 - 112 - taps)))
+    low, high = seg_bounds[0, :-1], seg_bounds[0, 1:]
+    bounds_two = jnp.stack([low, high], axis=1)
+    counts = (high - low).astype(F32)[None, :]
+    return kernel_rows, bounds_two, counts, seq_lengths.reshape(1, 1)
+
+
+def gelu_pair(hidden):
+    tail = jnp.exp(-0.5 * hidden * hidden)
+    t = 1.0 / (1.0 + 0.23164190 * jnp.abs(hidden))
+    poly = 1.330274429
+    for term in (-1.821255978, 1.781477937, -0.356563782, 0.319381530):
+        poly = poly * t + term
+    density = 0.3989422804014327 * tail
+    below = density * poly * t
+    normal = jnp.where(hidden >= 0.0, 1.0 - below, below)
+    return hidden * normal, normal + hidden * density
+
+
+def norm_forward(values):
+    center = jnp.mean(values, axis=-1, keepdims=True)
+    centred = values - center
+    spread = jnp.mean(centred * centred, axis=-1, keepdims=True)
+    root = lax.rsqrt(spread + 1e-5)
+    return centred * root, root
+
+
+def norm_backward(grad, gain, normed, root):
+    scaled = grad * gain
+    center = jnp.mean(scaled, axis=-1, keepdims=True)
+    along = jnp.mean(scaled * normed, axis=-1, keepdims=True)
+    return root * (scaled - center - normed * along)
+
+
+class Spread:
+    def __init__(self, acc, got, bits, sems, base):
+        self.acc, self.got, self.bits, self.sems, self.base = acc, got, bits, sems, base
+        self.blocks = acc.shape[0]
+        self.stage = 0
+        self.offset = 0
+        self.at = 0
+        self.flight = None
+        self.sent = []
+
+    def start(self):
+        bit, device = self.bits[self.stage]
+        size = self.blocks >> (self.stage + 1)
+        self.keep = self.offset + bit * size
+        other = self.offset + (1 - bit) * size
+        self.flight = copy_to(
+            self.acc.at[pl.ds(other, size)], self.got.at[pl.ds(self.at, size)],
+            self.sems, self.base + self.stage, device,
+        )
+        self.flight.start()
+        self.size = size
+
+    def take(self):
+        self.flight.wait_recv()
+        self.sent.append(self.flight)
+        mine, new = pl.ds(self.keep, self.size), pl.ds(self.at, self.size)
+        self.at += self.size
+        self.offset = self.keep
+        self.stage += 1
+        if self.stage == len(self.bits):
+            return self.acc[mine].astype(F32) + self.got[new].astype(F32)
+        self.acc[mine] = self.acc[mine] + self.got[new]
+        return None
+
+    def step(self):
+        self.take()
+        self.start()
+
+    def finish(self):
+        total = self.take()
+        for sent in self.sent:
+            sent.wait_send()
+        return total[0]
+
+
+def position(order, values):
+    spot = 0
+    for name in order:
+        spot = 2 * spot + values[name]
+    return spot
+
+
+DOWN_ORDERS = (("x", "y", "l", "h"), ("y", "x", "l", "h"), ("l", "x", "y", "h"))
+UP_ORDERS = (("y", "x", "l", "h"), ("l", "y", "x", "h"), ("x", "y", "l", "h"))
+OUT_ORDER = ("l", "x", "y", "h")
+QKV_ORDERS = (("y", "l", "h"), ("l", "y", "h"), ("y", "l", "h"))
+
+
+def backward_kernel(
+    tok_ref, grad_ref, gain_ref, shift_ref, heads_ref, all_ref, packed_ref, a1_ref, a3_ref,
+    n1_ref, n2_ref, marks_ref, kb_ref, bnd_ref, cnt_ref, len_ref,
+    wout_hbm, wup_hbm, wdown_hbm, wqkv_hbm,
+    out_ref, in_ref, gqkv_ref, gout_ref, gup_ref, gdown_ref, small_ref,
+    w_out, w_up, w_down, w_qkv, wsem, sems,
+    heads_x, low_t, low_x, act, gst, gst_x, slope, gh, gh_x, gb, gb_x, gatt, g_in, gproj, gp_in,
+    first_ref, norm1_ref, gr1_ref, sum_s, sum_r, fin,
+    acc_down, got_down, acc_up, got_up, acc_out, got_out, acc_qkv, got_qkv,
+):
+    dp = lax.axis_index("dp")
+    me = lax.axis_index("head")
+    quarters = 4
+    rows, width = tok_ref.shape
+    slot = rows * quarters
+    hidden_width = w_up.shape[1]
+    block = hidden_width // quarters
+    head_width = width // quarters
+    dim = 64
+    nh = head_width // dim
+    count = bnd_ref.shape[0]
+    band_rows = width // 8
+    down_cols = hidden_width // 8
+    core = lax.rem(me, 2)
+    mate = (dp, me ^ 1)
+    bits = {
+        "x": (lax.div(me, 2), (dp, me ^ 2)),
+        "y": (lax.rem(dp, 2), (dp ^ 1, me)),
+        "l": (lax.rem(lax.div(dp, 2), 2), (dp ^ 2, me)),
+        "h": (lax.div(dp, 4), (dp ^ 4, me)),
+    }
+    fetches = []
+    for i, (src, dst) in enumerate(
+        ((wout_hbm, w_out), (wup_hbm, w_up), (wdown_hbm, w_down), (wqkv_hbm, w_qkv))
+    ):
+        fetch = pltpu.make_async_copy(src, dst, wsem.at[i])
+        fetch.start()
+        fetches.append(fetch)
+    greet([(dp, me ^ k) for k in (1, 2, 3)] + [(dp ^ k, me) for k in (1, 2, 4)])
+    counter = iter(range(200))
+
+    def send(src, dst, device):
+        copy = copy_to(src, dst, sems, next(counter), device)
+        copy.start()
+        return copy
+
+    def reserve(n):
+        base = next(counter)
+        for _ in range(n - 1):
+            next(counter)
+        return base
+
+    def spread(acc, got, order):
+        return Spread(acc, got, [bits[name] for name in order], sems, reserve(len(order)))
+
+    heads_sent = send(heads_ref, heads_x, mate)
+    length = len_ref[...]
+    fetches[0].wait()
+    branch = mm(heads_ref[...], w_out[...], 0, 0)
+    normed, root_one = norm_forward(tok_ref[...].astype(F32) + branch)
+    norm1_ref[...] = normed
+    first = normed * gain_ref[0:1] + shift_ref[0:1]
+    first_ref[...] = first
+    low = first.astype(BF16)
+    low_t[...] = low.T
+    low_sent = send(low_t, low_x, mate)
+    fetches[1].wait()
+    fetches[2].wait()
+    second = None
+    act_sent = []
+    for i in range(quarters):
+        cols = slice(block * i, block * (i + 1))
+        active, slope_part = gelu_pair(mm(low, w_up[:, cols], 1, 0))
+        active = active.astype(BF16)
+        act[:rows, cols] = active
+        act_sent.append(send(act.at[:rows, cols], act.at[rows:, cols], mate))
+        slope[:, cols] = slope_part
+        part = mm(active, w_down[cols, :], 1, 0)
+        second = part if second is None else second + part
+    normed_two, root_two = norm_forward(first_ref[...] + second)
+    out_ref[...] = (normed_two * gain_ref[1:2] + shift_ref[1:2]).astype(BF16)
+    place = me * rows + lax.broadcasted_iota(jnp.int32, (rows, 1), 0)
+    cotangent = jnp.where(place < length, grad_ref[...].astype(F32), 0.0)
+    sum_s[0] = jnp.zeros(sum_s.shape[1:], F32)
+    sum_s[0, 1:2] = jnp.sum(cotangent * normed_two, axis=0, keepdims=True)
+    sum_s[0, 3:4] = jnp.sum(cotangent, axis=0, keepdims=True)
+    g_two = norm_backward(cotangent, gain_ref[1:2], normed_two, root_two)
+    gr1_ref[...] = g_two
+    g_low = g_two.astype(BF16)
+    gst[...] = g_low.T
+    gst_sent = send(gst, gst_x, mate)
+    for copy in act_sent:
+        copy.wait()
+    gst_sent.wait()
+    lead = jnp.concatenate(
+        [
+            jnp.concatenate(
+                [
+                    ref[pl.ds(pl.multiple_of(head_width * (2 * x + core), 64), head_width), :]
+                    for ref in (gst, gst_x)
+                ],
+                axis=1,
+            )
+            for x in range(2)
+        ],
+        axis=0,
+    )
+    for pair in range(4):
+        total = mm(lead, act[:, 2 * down_cols * pair : 2 * down_cols * (pair + 1)], 1, 0)
+        total = total.astype(BF16)
+        for x in range(2):
+            for inner in range(2):
+                values = {"x": x, "y": inner, "l": pair % 2, "h": pair // 2}
+                for q in range(3):
+                    top = head_width * x + 64 * q
+                    acc_down[q, position(DOWN_ORDERS[q], values)] = total[
+                        top : top + 64, down_cols * inner : down_cols * (inner + 1)
+                    ]
+    downs = [spread(acc_down.at[q], got_down.at[q], DOWN_ORDERS[q]) for q in range(3)]
+    for chunk in downs:
+        chunk.start()
+    g_first = gr1_ref[...]
+    gh_sent = []
+    for i in range(quarters):
+        cols = slice(block * i, block * (i + 1))
+        part = (slope[:, cols] * mm(g_low, w_down[cols, :], 1, 1)).astype(BF16)
+        gh[:, cols] = part
+        g_first = g_first + mm(part, w_up[:, cols], 1, 1)
+        if i % 2:
+            lanes = pl.ds(pl.multiple_of(block * (i - core), 128), block)
+            gh_sent.append(send(gh.at[:, lanes], gh_x.at[i // 2], mate))
+    normed = norm1_ref[...]
+    sum_s[0, 0:1] = jnp.sum(g_first * normed, axis=0, keepdims=True)
+    sum_s[0, 2:3] = jnp.sum(g_first, axis=0, keepdims=True)
+    g_one = norm_backward(g_first, gain_ref[0:1], normed, root_one)
+    gr1_ref[...] = g_one
+    g_branch = g_one.astype(BF16)
+    gb[...] = g_branch
+    gb_sent = send(gb, gb_x, mate)
+    gatt[...] = mm(w_out[...], g_branch, 1, 1).astype(BF16)
+    g_sent = []
+    mine = pl.ds(pl.multiple_of(rows * me, rows), rows)
+    for k in range(1, quarters):
+        src = gatt.at[pl.ds(pl.multiple_of(head_width * (me ^ k), 64), head_width)]
+        g_sent.append(send(src, g_in.at[:, mine], (dp, me ^ k)))
+    g_in[:, mine] = gatt[pl.ds(pl.multiple_of(head_width * me, 64), head_width)]
+    heads_sent.wait()
+    low_sent.wait()
+    for copy in gh_sent:
+        copy.wait()
+    gb_sent.wait()
+    lead = jnp.concatenate([low_t[...], low_x[...]], axis=1)
+    for x in range(2):
+        for q in range(3):
+            lanes = pl.ds(pl.multiple_of(block * (2 * x + core) + 256 * q, 128), 256)
+            side = jnp.concatenate([gh[:, lanes], gh_x[x, :, 256 * q : 256 * (q + 1)]], axis=0)
+            total = mm(lead, side, 1, 0).astype(BF16)
+            for d in range(8):
+                values = {"x": x, "y": d % 2, "l": d // 2 % 2, "h": d // 4}
+                acc_up[q, position(UP_ORDERS[q], values)] = total[
+                    band_rows * d : band_rows * (d + 1)
+                ]
+    ups = [spread(acc_up.at[q], got_up.at[q], UP_ORDERS[q]) for q in range(3)]
+    for chunk in ups:
+        chunk.start()
+    lead = jnp.concatenate([heads_ref[...], heads_x[...]], axis=1)
+    both = jnp.concatenate([gb[...], gb_x[...]], axis=0)
+    for x in range(2):
+        left_cols = both[:, 2 * head_width * x : 2 * head_width * x + head_width]
+        right_cols = both[:, 2 * head_width * x + head_width : 2 * head_width * (x + 1)]
+        total = mm(lead, jnp.where(core == 0, left_cols, right_cols), 1, 0).astype(BF16)
+        for d in range(8):
+            values = {"x": x, "y": d % 2, "l": d // 2 % 2, "h": d // 4}
+            acc_out[position(OUT_ORDER, values)] = total[band_rows * d : band_rows * (d + 1)]
+    outs = spread(acc_out, got_out, OUT_ORDER)
+    outs.start()
+    tokens_t = all_ref[...].T
+    for copy in g_sent:
+        copy.wait()
+    scale = dim ** (-0.25)
+    live = lax.broadcasted_iota(jnp.int32, (1, slot), 1) < length
+    member = members(bnd_ref, slot)
+    unit = eye(count)
+    flip_rows = lax.broadcasted_iota(jnp.int32, (128, 128), 0)
+    flip_cols = lax.broadcasted_iota(jnp.int32, (128, 128), 1)
+    flip = (flip_rows + flip_cols == 127).astype(F32).astype(BF16)
+    starts = []
+    kept = []
+    for head in range(nh):
+        at = dim * head
+        grad = jnp.where(live, g_in[at : at + dim].astype(F32), 0.0).astype(BF16)
+        values = packed_ref[2 * head_width + at : 2 * head_width + at + dim]
+        values = jnp.where(live, values.astype(F32), 0.0).astype(BF16)
+        first = a1_ref[head]
+        third = a3_ref[head]
+        summary, inverse = marks_ref[head, 3], marks_ref[head, 5]
+        f_high, f_low = halves(first)
+        g_weights = mm(jnp.concatenate([f_high, f_low], axis=0), grad, 1, 1)
+        g_weights = g_weights[:count] + g_weights[count:]
+        starts.append((fine(g_weights, summary.T), jnp.zeros((count, count), F32)))
+        g_summary = fine(inverse.T, g_weights)
+        gt_high, gt_low = halves(g_summary.T)
+        t_high, t_low = halves(third)
+        g_values = mm(
+            jnp.concatenate([gt_high, gt_high, gt_low], axis=1),
+            jnp.concatenate([t_high, t_low, t_high], axis=0), 1, 0,
+        )
+        g_wide = windows(grad)
+        g_values = g_values + unwindow(mm(g_wide, toeplitz(kb_ref[head, 1:2]), 1, 1), dim)
+        gproj[2 * head_width + at : 2 * head_width + at + dim] = jnp.where(
+            live, g_values, 0.0
+        ).astype(BF16)
+        turned = mm(g_wide[:, 128:256], flip, 1, 0).astype(BF16)
+        gram = mm(turned, windows(values), 0, 0)
+        gram = pltpu.roll(gram, 384 - 127, 1, stride=1, stride_axis=0)
+        taps = pltpu.roll(jnp.sum(gram, axis=0, keepdims=True), 384 - 112, 1)
+        lane = lax.broadcasted_iota(jnp.int32, taps.shape, 1)
+        sum_s[0, pl.ds(4 + nh * me + head, 1), 0:384] = jnp.where(lane < 33, taps, 0.0)
+        kept.append((grad, values, g_summary))
+    p_sent = []
+
+    def share(part):
+        for k in range(1, quarters):
+            lanes = pl.ds(pl.multiple_of(rows * (me ^ k), rows), rows)
+            src = gproj.at[head_width * part : head_width * (part + 1), lanes]
+            dst = gp_in.at[
+                pl.ds(pl.multiple_of(width * part + head_width * me, 64), head_width)
+            ]
+            p_sent.append(send(src, dst, (dp, me ^ k)))
+        gp_in[pl.ds(pl.multiple_of(width * part + head_width * me, 64), head_width)] = gproj[
+            head_width * part : head_width * (part + 1), mine
+        ]
+
+    projs = [spread(acc_qkv.at[j], got_qkv.at[j], QKV_ORDERS[j]) for j in range(3)]
+
+    def qkv_gradient(part):
+        total = mm(tokens_t, gproj[head_width * part : head_width * (part + 1)], 1, 1)
+        total = total.astype(BF16)
+        for d in range(8):
+            values = {"y": d % 2, "l": d // 2 % 2, "h": d // 4}
+            acc_qkv[part, position(QKV_ORDERS[part], values)] = total[
+                band_rows * d : band_rows * (d + 1)
+            ]
+        projs[part].start()
+
+    share(2)
+    qkv_gradient(2)
+    sums = []
+    for k, name in enumerate(("c", "x", "y", "l", "h")):
+        sums.append((mate if name == "c" else bits[name][1]))
+    sum_base = reserve(5)
+
+    def sum_start(k):
+        copy = copy_to(sum_s.at[k], sum_r.at[k], sems, sum_base + k, sums[k])
+        copy.start()
+        return copy
+
+    def sum_step(k, copy):
+        copy.wait()
+        total = sum_s[k] + sum_r[k]
+        if k == 4:
+            small_ref[...] = total
+            return None
+        sum_s[k + 1] = total
+        return sum_start(k + 1)
+
+    pending = sum_start(0)
+    for chunk in downs:
+        chunk.step()
+
+    def newton(index, carry):
+        step = NEWTON - 1 - index
+        out = []
+        for head in range(nh):
+            outer, hold = carry[head]
+            pair_one, pair_two = n1_ref[head, step], n2_ref[head, step]
+            product, second = pair_one[:, :count], pair_one[:, count:]
+            third, inverse = pair_two[:, :count], pair_two[:, count:]
+            blend = 0.25 * (13.0 * unit - 15.0 * product + 7.0 * second - third)
+            left_p, left_s = left(product), left(second)
+            inner = fine(inverse.T, outer)
+            by_hold = mm(jnp.concatenate([left_p, left_s, left(third)], axis=0), right(hold), 1, 0)
+            by_inner = mm(jnp.concatenate([left_p, left_s], axis=0), right(inner), 1, 0)
+            zero_th = inner + by_hold[:count]
+            once = by_inner[:count] + by_hold[count : 2 * count]
+            twice = by_inner[count:] + by_hold[2 * count :]
+            both = mm(jnp.concatenate([left(outer), left(hold)], axis=0), right(blend), 1, 0)
+            rest = fine(zero_th, 7.0 * product - second - 15.0 * unit)
+            rest = rest + fine(once, 7.0 * unit - product) - twice
+            out.append((both[:count], both[count:] + 0.25 * rest))
+        return tuple(out)
+
+    ends = lax.fori_loop(0, NEWTON, newton, tuple(starts))
+    pending = sum_step(0, pending)
+    for chunk in downs:
+        chunk.step()
+    for chunk in ups:
+        chunk.step()
+    outs.step()
+    for head in range(nh):
+        at = dim * head
+        grad, values, g_summary = kept[head]
+        q_marks, k_marks, middle = marks_ref[head, 0], marks_ref[head, 1], marks_ref[head, 2]
+        weights = marks_ref[head, 4]
+        queries = packed_ref[at : at + dim]
+        keys = packed_ref[head_width + at : head_width + at + dim]
+        first = a1_ref[head]
+        third = a3_ref[head]
+        w_high, w_low = halves(weights)
+        g_first_a = mm(
+            jnp.concatenate([w_high, w_low], axis=1), jnp.concatenate([grad, grad], axis=0), 1, 0
+        )
+        g_one_s = first * (g_first_a - jnp.sum(g_first_a * first, axis=0, keepdims=True))
+        s_high, s_low = halves(g_summary)
+        g_third = mm(
+            jnp.concatenate([s_high, s_low], axis=1),
+            jnp.concatenate([values, values], axis=0), 1, 0,
+        )
+        g_three_s = third * (g_third - jnp.sum(g_third * third, axis=1, keepdims=True))
+        one_high, one_low = halves(g_one_s)
+        three_high, three_low = halves(g_three_s)
+        g_k_marks = mm(jnp.concatenate([one_high, one_low], axis=0), queries, 1, 1)
+        g_k_marks = (g_k_marks[:count] + g_k_marks[count:]) * scale
+        g_q_marks = mm(jnp.concatenate([three_high, three_low], axis=0), keys, 1, 1)
+        g_q_marks = (g_q_marks[:count] + g_q_marks[count:]) * scale
+        outer, hold = ends[head]
+        inverse = n2_ref[head, 0][:, count:]
+        col_sums = jnp.sum(middle, axis=0, keepdims=True)
+        row_sums = jnp.sum(middle, axis=1, keepdims=True)
+        col_top = jnp.max(col_sums, axis=1, keepdims=True)
+        row_top = jnp.max(row_sums, axis=0, keepdims=True)
+        g_start = outer + fine(middle.T, hold)
+        g_norm = -jnp.sum(
+            jnp.sum(g_start * inverse, axis=1, keepdims=True), axis=0, keepdims=True
+        ) / (col_top * row_top)
+        col_hit = (col_sums == col_top).astype(F32)
+        row_hit = (row_sums == row_top).astype(F32)
+        col_hit = col_hit / jnp.sum(col_hit, axis=1, keepdims=True)
+        row_hit = row_hit / jnp.sum(row_hit, axis=0, keepdims=True)
+        g_middle = fine(hold, inverse.T) + g_start.T / (col_top * row_top)
+        g_middle = g_middle + g_norm * (row_top * col_hit + col_top * row_hit)
+        g_two_s = middle * (g_middle - jnp.sum(g_middle * middle, axis=1, keepdims=True))
+        g_q_marks = g_q_marks + fine(g_two_s, k_marks)
+        g_k_marks = g_k_marks + fine(g_two_s.T, q_marks)
+        share_of = 1.0 / cnt_ref[...]
+        for base, marks, g_marks, high in (
+            (at, k_marks, g_q_marks, one_high),
+            (head_width + at, q_marks, g_k_marks, three_high),
+        ):
+            m_high, m_low = halves(marks.T)
+            l_high, l_low = halves(g_marks.T * share_of)
+            total = mm(
+                jnp.concatenate([m_high, m_low, l_high, l_low], axis=1),
+                jnp.concatenate([high, high, member, member], axis=0), 1, 0,
+            )
+            gproj[base : base + dim] = (total * scale).astype(BF16)
+    share(0)
+    share(1)
+    qkv_gradient(0)
+    qkv_gradient(1)
+    pending = sum_step(1, pending)
+    for chunk in ups:
+        chunk.step()
+    outs.step()
+    for chunk in downs:
+        chunk.step()
+    projs[2].step()
+    fetches[3].wait()
+    for copy in p_sent:
+        copy.wait()
+    in_ref[...] = (gr1_ref[...] + mm(gp_in[...], w_qkv[...], 0, 1)).astype(BF16)
+    pending = sum_step(2, pending)
+    projs[0].step()
+    projs[1].step()
+    for chunk in ups:
+        chunk.step()
+    outs.step()
+    for q in range(3):
+        gdown_ref[64 * q : 64 * (q + 1)] = downs[q].finish()
+    pending = sum_step(3, pending)
+    projs[2].step()
+    projs[0].step()
+    projs[1].step()
+    for q in range(3):
+        gup_ref[:, 256 * q : 256 * (q + 1)] = ups[q].finish()
+    gout_ref[...] = outs.finish()
+    sum_step(4, pending)
+    last = reserve(3)
+    for part in (2, 0, 1):
+        total = projs[part].finish()
+        spot = quarters * part + me
+        dest, where = lax.div(spot, 3), lax.rem(spot, 3)
+
+        @pl.when(dest == me)
+        def _():
+            gqkv_ref[where] = total
+
+        @pl.when(dest != me)
+        def _():
+            fin[part] = total
+            pltpu.make_async_remote_copy(
+                src_ref=fin.at[part], dst_ref=gqkv_ref.at[where],
+                send_sem=sems.at[0, last + part], recv_sem=sems.at[1, last + where],
+                device_id=(dp, dest), device_id_type=MESH,
+            ).start()
+
+    for index in range(3):
+        spot = quarters * index + me
+        source = lax.rem(3 * me + index, quarters)
+
+        @pl.when(lax.div(spot, 3) != me)
+        def _():
+            copy_to(fin.at[index], gqkv_ref.at[0], sems, last + index, mate).wait_send()
+
+        @pl.when(source != me)
+        def _():
+            copy_to(fin.at[0], gqkv_ref.at[index], sems, last + index, mate).wait_recv()
+
+
+def backward_call(tokens, out_grad, gains, shifts, forward, small, w_out, w_up, w_down, w_qkv):
+    heads, everyone, packed, a1, a3, n1, n2, marks = forward
+    kernel_rows, bounds_two, counts, length = small
+    rows, width = tokens.shape
+    ff = w_up.shape[1]
+    nh = kernel_rows.shape[0]
+    head_width = nh * 64
+    band_rows, down_cols = width // 8, ff // 8
+    whole = pl.BlockSpec(memory_space=VMEM)
+    anywhere = pl.BlockSpec(memory_space=pl.ANY)
+    shape = jax.ShapeDtypeStruct
+    return pl.pallas_call(
+        backward_kernel,
+        out_shape=(
+            shape((rows, width), BF16),
+            shape((rows, width), BF16),
+            shape((3, band_rows, head_width), F32),
+            shape((band_rows, head_width), F32),
+            shape((band_rows, ff // 4), F32),
+            shape((head_width, down_cols), F32),
+            shape((16, width), F32),
+        ),
+        in_specs=[whole] * 16 + [anywhere] * 4,
+        out_specs=[whole] * 7,
+        scratch_shapes=[
+            VMEM(w_out.shape, BF16), VMEM(w_up.shape, BF16), VMEM(w_down.shape, BF16),
+            VMEM(w_qkv.shape, BF16), pltpu.SemaphoreType.DMA((4,)),
+            pltpu.SemaphoreType.DMA((2, 96)),
+            VMEM((width, rows), BF16),
+            VMEM((width, rows), BF16), VMEM((width, rows), BF16),
+            VMEM((2 * rows, ff), BF16),
+            VMEM((width, rows), BF16), VMEM((width, rows), BF16),
+            VMEM((rows, ff), F32),
+            VMEM((rows, ff), BF16), VMEM((2, rows, ff // 4), BF16),
+            VMEM((rows, width), BF16), VMEM((rows, width), BF16),
+            VMEM((width, rows), BF16),
+            VMEM((head_width, 4 * rows), BF16),
+            VMEM((3 * head_width, 4 * rows), BF16),
+            VMEM((3 * width, rows), BF16),
+            VMEM((rows, width), F32), VMEM((rows, width), F32), VMEM((rows, width), F32),
+            VMEM((5, 16, width), F32), VMEM((5, 16, width), F32),
+            VMEM((3, band_rows, head_width), F32),
+            VMEM((3, 16, 64, down_cols), BF16), VMEM((3, 15, 64, down_cols), BF16),
+            VMEM((3, 16, band_rows, 256), BF16), VMEM((3, 15, band_rows, 256), BF16),
+            VMEM((16, band_rows, head_width), BF16), VMEM((15, band_rows, head_width), BF16),
+            VMEM((3, 8, band_rows, head_width), BF16), VMEM((3, 7, band_rows, head_width), BF16),
+        ],
+        compiler_params=pltpu.CompilerParams(
+            collective_id=1, has_side_effects=True, vmem_limit_bytes=62 * 2**20
+        ),
+    )(
+        tokens, out_grad, gains, shifts, heads.reshape(width, rows),
+        everyone.reshape(4 * rows, width), packed, a1, a3, n1, n2, marks,
+        kernel_rows, bounds_two, counts, length, w_out, w_up, w_down, w_qkv,
+    )
+
+
+def per_device_fast(
+    tokens, w_qkv, w_out, w_up, w_down, norm_gains, norm_shifts, conv_kernels, seq_lengths,
+    seg_bounds, out_grad,
+):
+    quarters = lax.axis_size("head")
+    heads, taps = conv_kernels.shape
+    small = small_inputs(conv_kernels, seq_lengths, seg_bounds, lax.axis_index("head"), heads // quarters)
+    forward = forward_call(tokens, w_qkv, *small, quarters)
+    out, in_grad, g_qkv, g_out, g_up, g_down, sums = backward_call(
+        tokens, out_grad, norm_gains, norm_shifts, forward, small, w_out, w_up, w_down, w_qkv
+    )
+    g_qkv = g_qkv.transpose(1, 0, 2).reshape(g_qkv.shape[1], -1)
+    return (
+        out, in_grad, g_qkv, g_out, g_up, g_down.T, sums[0:2], sums[2:4],
+        sums[4 : 4 + heads, :taps],
+    )
 
 
 highest = lax.Precision.HIGHEST
@@ -243,8 +1095,9 @@
         P("dp", None),
         P(("dp", "head"), None),
     )
+    aligned = mesh.shape["dp"] == 8 and mesh.shape["head"] == 4
     return jax.shard_map(
-        per_device,
+        per_device_fast if aligned else per_device,
         mesh=mesh,
         in_specs=placed,
         out_specs=(

time: 718 us -> 155 us (0.22); the launches traced: 708 us -> 154 us
  waiting for transfers between devices: 296 us -> 0 us
  Pallas kernels: 0 us -> 132 us
  local copies, waits for them, and re-layouts: 138 us -> 19.4 us
  matrix products: 103 us -> 0 us
  blocking collectives: 73.4 us -> 0 us
  other arithmetic: 66.2 us -> 1.6 us
  between operations: 18.1 us -> 1.35 us
  starting transfers between devices: 12.7 us -> 0 us
    reduce_scatter x4 -> x0, waiting for transfers between devices: 280 us -> none  [the longest x1 141 us: per_device(): lax.psum_scatter(blocked_down, ('dp', 'head'), scatter_dimension=0, tiled...]
    pallas_call x0 -> x2, Pallas kernels: none -> 132 us  [the longest x1 98.9 us: backward_call(): pl.pallas_call(backward_kernel, out_shape=(shape((rows, width), BF16), sh...]
    dot_general x106 -> x0, matrix products: 103 us -> none  [the longest x4 18.4 us: row_contract(): lax.dot_general(left, right, (((0,), (0,)), ((), ())), preferred_element_...]
    psum x1 -> x0, blocking collectives: 41.2 us -> none  [per_device(): lax.psum((jnp.stack([grad_gain_one, grad_gain_two]), jnp.stack([grad_shif...]
    reshape x8 -> x0, local copies, waits for them, and re-layouts: 38 us -> none  [the longest x2 23.3 us: to_blocks(): matrix.reshape(dp_count, total_rows // dp_count, quarters, total_cols //...]
    all_to_all x1 -> x0, blocking collectives: 32.3 us -> none  [per_device(): lax.all_to_all(grad_packed_low, 'head', split_axis=0, concat_axis=2, tile...]
    reduce_sum x11 -> x0, other arithmetic: 29.8 us -> none  [the longest x2 21.9 us: shifted_conv(): total = total + kernel[offset] * padded[offset:offset + slot_len]]
    transpose x3 -> x1, local copies, waits for them, and re-layouts: 30.9 us -> 1.11 us  [per_device_fast(): g_qkv = g_qkv.transpose(1, 0, 2).reshape(g_qkv.shape[1], -1)]
  transfers between devices with their start and end apart: 7 -> 0, of which waited for: 5 -> 0; matrix products, arithmetic and copies ran while one was open for 28% -> 0% of each run, Pallas kernels for 0% -> 0%
where the time goes in v1:
time: 155 us; the launch traced here: 154 us
  Pallas kernels  132 us (85%)
  local copies, waits for them, and re-layouts  19.4 us (13%)
  other arithmetic  1.6 us (1%)
    pallas_call x1, Pallas kernels, backward_call(): pl.pallas_call(backward_kernel, out_shape=(shape((rows, width), BF16), sh...  98.9 us
    pallas_call x1, Pallas kernels, forward_call(): pl.pallas_call(forward_kernel, out_shape=(jax.ShapeDtypeStruct((quarters,...  33.2 us
    unnamed x30, local copies, waits for them, and re-layouts  15.4 us

profile of v1, /device:TPU:0, one launch (start us, length us, event | category | flops | bytes accessed | tf_op | source)
XLA Modules:
  0.0 154.5 jit_solution(7495360341430458747)
XLA Ops:
  1.3 0.8 subtract_convert_fusion
  2.1 0.7 fusion
  2.8 0.1 rev.3
  2.9 0.1 select_maximum_fusion.kb_ref
  3.0 0.1 copy.32.bnd_ref
  3.1 1.0 copy-done
  4.1 33.2 %shard_map.178 = (bf16[4,192,256]{2,1,0:T(8,128)(2,1)S(1)}, bf16[4,256,768]{2,1,0:T(8,128)(2,1)}, bf16[576,1024]{1,0:T(8,128)(2,1)S(1)}, f32[3,64,1024]{2,1,0:T(...) custom-call(bf16[256,768]{1,0:T(8,128)(2,1)S(1)} %copy-done, ...), custom_call_target="tpu_custom_call" | custom-call | tf_op jit(solution)/shard_map/pallas_call | solution.py:244
  37.3 1.0 copy-done.1
  38.3 0.9 copy-done.2
  39.2 0.9 copy-done.3
  40.1 0.8 copy-done.4
  40.9 0.8 copy-done.5
  41.7 0.8 copy-done.6
  42.6 0.7 copy-done.7
  43.3 98.9 %shard_map.179 = (bf16[256,768]{1,0:T(8,128)(2,1)}, bf16[256,768]{1,0:T(8,128)(2,1)}, f32[3,96,192]{2,1,0:T(8,128)}, f32[96,192]{1,0:T(8,128)}, f32[96,768]{1,0:...) custom-call(bf16[256,768]{1,0:T(8,128)(2,1)} %tok_ref.3, bf16[256,768]{1,0:T(8,128)(2,1)} %grad_ref.1, ...), custom_call_target="tpu_custom_call" | custom-call | tf_op jit(solution)/shard_map/pallas_call | solution.py:797
  142.3 1.3 slice.19
  143.6 1.4 fusion.1
  145.0 1.1 copy.34
  146.1 0.9 copy.35
  147.0 1.8 %copy.42 = bf16[256,768]{1,0:T(8,128)(2,1)} copy(bf16[256,768]{1,0:T(8,128)(2,1)} %get-tuple-element.73) | data formatting | bytes 786432
  148.8 1.8 %copy.43 = bf16[256,768]{1,0:T(8,128)(2,1)} copy(bf16[256,768]{1,0:T(8,128)(2,1)} %get-tuple-element.74) | data formatting | bytes 786432
  150.5 1.5 copy.44
  152.1 1.7 %copy.45 = f32[96,768]{1,0:T(8,128)} copy(f32[96,768]{1,0:T(8,128)} %get-tuple-element.77) | data formatting | bytes 589824
  153.8 0.7 copy.46
  (19 shorter events, 0.0 us)
Async XLA Ops:
  2.1 41.2 %copy-start.10 = (f32[1,64]{1,0:T(1,128)}, f32[1,64]{1,0:T(1,128)S(1)}, u32[]{:S(2)}) copy-start(f32[1,64]{1,0:T(1,128)S(1)} %get-tuple-element.61.cnt_ref) | copy-start | bytes 772
  3.0 40.3 %copy-start.9 = (f32[3,2,384]{2,1,0:T(2,128)}, f32[3,2,384]{2,1,0:T(2,128)S(1)}, u32[]{:S(2)}) copy-start(f32[3,2,384]{2,1,0:T(2,128)S(1)} %select_maximum_fusion.kb_ref) | copy-start | bytes 27652
  3.1 1.0 copy-start
  4.1 39.2 %copy-start.8 = (s32[64,2]{1,0:T(8,128)}, s32[64,2]{1,0:T(8,128)S(1)}, u32[]{:S(2)}) copy-start(s32[64,2]{1,0:T(8,128)S(1)} %copy.32.bnd_ref) | copy-start | bytes 1540
  37.3 1.0 copy-start.1
  38.3 0.9 copy-start.2
  39.2 0.9 copy-start.3
  40.1 0.8 copy-start.4
  40.9 0.8 copy-start.5
  41.7 0.8 copy-start.6
  42.6 0.7 copy-start.7
  142.3 11.5 %copy-start.11 = (f32[192,384]{1,0:T(8,128)S(1)}, f32[192,384]{1,0:T(8,128)}, u32[]{:S(2)}) copy-start(f32[192,384]{1,0:T(8,128)} %get-tuple-element.37) | copy-start | bytes 884740

commit v2 on v0

--- a/solution.py
+++ b/solution.py
@@ -2,8 +2,825 @@
 import jax.numpy as jnp
 from jax import lax
 from jax.sharding import PartitionSpec as P
-
+from jax.experimental import pallas as pl
+from jax.experimental.pallas import tpu as pltpu
+
+MESH = pl.DeviceIdType.MESH
 NEWTON = 6
+F32 = jnp.float32
+BF16 = jnp.bfloat16
+VMEM = pltpu.VMEM
+HEADS_HERE = 3
+DIM = 64
+TAPS = 33
+
+
+def mm(a, b, ca, cb):
+    return lax.dot_general(a, b, (((ca,), (cb,)), ((), ())), preferred_element_type=F32)
+
+
+def halves(value):
+    high = value.astype(BF16)
+    return high, (value - high.astype(F32)).astype(BF16)
+
+
+def cat(parts, axis):
+    return jnp.concatenate(parts, axis=axis)
+
+
+class Packs:
+    def __init__(self):
+        lane = lax.broadcasted_iota(jnp.int32, (1, HEADS_HERE * DIM), 1)
+        self.hit = [(lane // DIM == h).astype(F32) for h in range(HEADS_HERE)]
+        self.low_hit = [h.astype(BF16) for h in self.hit]
+        rows = lax.broadcasted_iota(jnp.int32, (DIM, HEADS_HERE * DIM), 0)
+        cols = lax.broadcasted_iota(jnp.int32, (DIM, HEADS_HERE * DIM), 1)
+        self.unit = (rows == cols % DIM).astype(F32)
+
+    def block(self, low):
+        return cat([low * h for h in self.low_hit], 0)
+
+    def times(self, lhs, rhs, side=0):
+        rows = lhs.shape[0]
+        l_high, l_low = halves(lhs)
+        r_high, r_low = halves(rhs)
+        both = mm(cat([l_high, l_low], 0), self.block(r_high), 1, side)
+        return both[:rows] + both[rows:] + mm(l_high, self.block(r_low), 1, side)
+
+    def diagonal(self, full):
+        total = full[:DIM] * self.hit[0]
+        for h in range(1, HEADS_HERE):
+            total = total + full[DIM * h : DIM * (h + 1)] * self.hit[h]
+        return total
+
+    def turn(self, value):
+        tall = value.T
+        return cat([tall[DIM * h : DIM * (h + 1)] for h in range(HEADS_HERE)], 1)
+
+    def each(self, values):
+        total = values[0] * self.hit[0]
+        for h in range(1, HEADS_HERE):
+            total = total + values[h] * self.hit[h]
+        return total
+
+    def row_max(self, value):
+        return self.each(
+            [
+                jnp.max(jnp.where(h > 0, value, -jnp.inf), axis=1, keepdims=True)
+                for h in self.hit
+            ]
+        )
+
+    def row_sum(self, value):
+        return self.each([jnp.sum(value * h, axis=1, keepdims=True) for h in self.hit])
+
+
+def expand(block_low, lhs_side, wide):
+    return mm(block_low, wide, lhs_side, 0)
+
+
+def toeplitz(base):
+    rows = jnp.broadcast_to(base, (128, base.shape[1]))
+    return pltpu.roll(rows, 0, 1, stride=1, stride_axis=0).astype(BF16)
+
+
+def windows(mat):
+    zero = jnp.zeros((mat.shape[0], 128), mat.dtype)
+    wide = cat([zero, mat, zero], 1)
+    return cat([wide[:, 128 * b : 128 * b + 384] for b in range(mat.shape[1] // 128)], 0)
+
+
+def unwindow(stacked, rows):
+    return cat([stacked[rows * b : rows * (b + 1)] for b in range(stacked.shape[0] // rows)], 1)
+
+
+def gelu_pair(hidden):
+    tail = jnp.exp(-0.5 * hidden * hidden)
+    t = 1.0 / (1.0 + 0.23164190 * jnp.abs(hidden))
+    poly = 1.330274429
+    for term in (-1.821255978, 1.781477937, -0.356563782, 0.319381530):
+        poly = poly * t + term
+    density = 0.3989422804014327 * tail
+    below = density * poly * t
+    normal = jnp.where(hidden >= 0.0, 1.0 - below, below)
+    return hidden * normal, normal + hidden * density
+
+
+def norm_forward(values):
+    center = jnp.mean(values, axis=-1, keepdims=True)
+    centred = values - center
+    spread = jnp.mean(centred * centred, axis=-1, keepdims=True)
+    root = lax.rsqrt(spread + 1e-5)
+    return centred * root, root
+
+
+def norm_backward(grad, gain, normed, root):
+    scaled = grad * gain
+    center = jnp.mean(scaled, axis=-1, keepdims=True)
+    along = jnp.mean(scaled * normed, axis=-1, keepdims=True)
+    return root * (scaled - center - normed * along)
+
+
+def copy_to(src, dst, sems, index, device):
+    return pltpu.make_async_remote_copy(
+        src_ref=src,
+        dst_ref=dst,
+        send_sem=sems.at[0, index],
+        recv_sem=sems.at[1, index],
+        device_id=device,
+        device_id_type=MESH,
+    )
+
+
+def greet(devices):
+    barrier = pltpu.get_barrier_semaphore()
+    for device in devices:
+        pl.semaphore_signal(barrier, inc=1, device_id=device, device_id_type=MESH)
+    pl.semaphore_wait(barrier, len(devices))
+
+
+class Spread:
+    def __init__(self, acc, got, bits, sems, base):
+        self.acc, self.got, self.bits, self.sems, self.base = acc, got, bits, sems, base
+        self.blocks = acc.shape[0]
+        self.stage = 0
+        self.offset = 0
+        self.at = 0
+        self.sent = []
+
+    def start(self):
+        bit, device = self.bits[self.stage]
+        size = self.blocks >> (self.stage + 1)
+        self.keep = self.offset + bit * size
+        other = self.offset + (1 - bit) * size
+        self.flight = copy_to(
+            self.acc.at[pl.ds(other, size)], self.got.at[pl.ds(self.at, size)],
+            self.sems, self.base + self.stage, device,
+        )
+        self.flight.start()
+        self.size = size
+
+    def take(self):
+        self.flight.wait_recv()
+        self.sent.append(self.flight)
+        mine, new = pl.ds(self.keep, self.size), pl.ds(self.at, self.size)
+        self.at += self.size
+        self.offset = self.keep
+        self.stage += 1
+        if self.stage == len(self.bits):
+            return self.acc[mine].astype(F32) + self.got[new].astype(F32)
+        self.acc[mine] = self.acc[mine] + self.got[new]
+        return None
+
+    def step(self):
+        self.take()
+        self.start()
+
+    def finish(self):
+        total = self.take()
+        for sent in self.sent:
+            sent.wait_send()
+        return total[0]
+
+
+def position(order, values):
+    spot = 0
+    for name in order:
+        spot = 2 * spot + values[name]
+    return spot
+
+
+DOWN_ORDERS = (("x", "y", "l", "h"), ("y", "l", "x", "h"), ("l", "y", "x", "h"))
+UP_ORDERS = (("y", "l", "x", "h"), ("l", "y", "x", "h"), ("x", "l", "y", "h"))
+OUT_ORDER = ("y", "l", "x", "h")
+QKV_ORDERS = (("y", "l", "h"), ("l", "y", "h"), ("l", "y", "h"))
+
+
+def main_kernel(
+    tok_hbm, grad_hbm, wqkv_hbm, wout_hbm, wup_hbm, wdown_hbm,
+    gain_ref, shift_ref, taps_ref, len_ref, bounds_ref,
+    out_hbm, in_hbm, gqkv_hbm, gout_hbm, gup_hbm, gdown_hbm, ggain_hbm, gshift_hbm, gtaps_hbm,
+    tok, grad_in, w_qkv, w_out, w_up, w_down, lsem, sems,
+    everyone, wt, bases, packed, a1, a3, chain, marks, att, heads, heads_x,
+    low_t, low_x, act, gst, gst_x, slope, gh, gh_x, gb, gb_x, gatt, g_in, gproj, gp_in,
+    first_ref, norm1_ref, gr1_ref, sum_s, sum_r, fin, slots,
+    acc_down, got_down, acc_up, got_up, acc_out, got_out, acc_qkv, got_qkv,
+    out_v, in_v, gqkv_v, gout_v, gup_v, gdown_v, ggain_v, gshift_v, gtaps_v,
+):
+    dp = lax.axis_index("dp")
+    me = lax.axis_index("head")
+    quarters = 4
+    rows, width = tok.shape
+    slot = rows * quarters
+    hidden_width = w_up.shape[1]
+    block = hidden_width // quarters
+    head_width = width // quarters
+    count = DIM
+    nh = HEADS_HERE
+    band_rows = width // 8
+    down_cols = hidden_width // 8
+    core = lax.rem(me, 2)
+    mate = (dp, me ^ 1)
+    bits = {
+        "x": (lax.div(me, 2), (dp, me ^ 2)),
+        "y": (lax.rem(dp, 2), (dp ^ 1, me)),
+        "l": (lax.rem(lax.div(dp, 2), 2), (dp ^ 2, me)),
+        "h": (lax.div(dp, 4), (dp ^ 4, me)),
+    }
+    counter = iter(range(200))
+    local = iter(range(40))
+
+    def fetch(src, dst):
+        copy = pltpu.make_async_copy(src, dst, lsem.at[next(local)])
+        copy.start()
+        return copy
+
+    def send(src, dst, device):
+        copy = copy_to(src, dst, sems, next(counter), device)
+        copy.start()
+        return copy
+
+    def reserve(n):
+        base = next(counter)
+        for _ in range(n - 1):
+            next(counter)
+        return base
+
+    def spread(acc, got, order):
+        return Spread(acc, got, [bits[name] for name in order], sems, reserve(len(order)))
+
+    own_fetch = fetch(tok_hbm, everyone.at[me])
+    tok_fetch = fetch(tok_hbm, tok)
+    wqkv_fetch = fetch(wqkv_hbm, w_qkv)
+    wout_fetch = fetch(wout_hbm, w_out)
+    wup_fetch = fetch(wup_hbm, w_up)
+    wdown_fetch = fetch(wdown_hbm, w_down)
+    grad_fetch = fetch(grad_hbm, grad_in)
+    greet([(dp, me ^ k) for k in (1, 2, 3)] + [(dp ^ k, me) for k in (1, 2, 4)])
+    half = rows // 2
+    far = []
+    for piece in range(2):
+        part = pl.ds(piece * half, half)
+        far.append(send(tok_hbm.at[part], everyone.at[me, part], (dp, me ^ 2)))
+    near = send(tok_hbm, everyone.at[me], mate)
+    wqkv_fetch.wait()
+    odd = lax.rem(me, 2)
+    for part in range(3):
+        start = pl.multiple_of(part * width + 2 * head_width * lax.div(me, 2) + 128 * odd, 128)
+        wt[part] = w_qkv[:, pl.ds(start, 256)].T
+    w_own = cat(
+        [wt[part, pl.ds(pl.multiple_of(64 * odd, 64), head_width), :] for part in range(3)], 0
+    )
+    packs = Packs()
+    lane = lax.broadcasted_iota(jnp.int32, (TAPS, 384), 1)
+    tap = lax.broadcasted_iota(jnp.int32, (TAPS, 384), 0)
+    for turn, spots in enumerate((tap + 112, 144 - tap)):
+        bases[turn] = mm(taps_ref[...], (lane == spots).astype(F32).astype(BF16), 1, 0)
+    bands = [
+        [toeplitz(bases[turn, pl.ds(nh * me + h, 1), :]) for h in range(nh)] for turn in range(2)
+    ]
+    edges = bounds_ref[...].astype(F32)
+    low_edge = jnp.broadcast_to(edges[:, :count], (count, count)).T[:, 0:1]
+    high_edge = jnp.broadcast_to(edges[:, 1 : count + 1], (count, count)).T[:, 0:1]
+    place = lax.broadcasted_iota(jnp.int32, (count, slot), 1).astype(F32)
+    member = ((place >= low_edge) & (place < high_edge)).astype(F32).astype(BF16)
+    share_of = 1.0 / (high_edge - low_edge)
+    length = len_ref[0]
+    live = lax.broadcasted_iota(jnp.int32, (1, slot), 1) < length
+    scale = DIM ** (-0.25)
+
+    def project(which):
+        lanes = pl.ds(pl.multiple_of(rows * which, rows), rows)
+        packed[:, lanes] = mm(w_own, everyone[which], 1, 1).astype(BF16)
+
+    own_fetch.wait()
+    project(me)
+    near.wait()
+    project(me ^ 1)
+    onward = []
+    for piece in range(2):
+        part = pl.ds(piece * half, half)
+        far[piece].wait()
+        onward.append(send(everyone.at[me ^ 2, part], everyone.at[me ^ 2, part], mate))
+    project(me ^ 2)
+    for copy in onward:
+        copy.wait()
+    project(me ^ 3)
+    queries = packed[:head_width]
+    keys = packed[head_width : 2 * head_width]
+    q_marks = mm(member, queries, 1, 1) * (scale * share_of)
+    k_marks = mm(member, keys, 1, 1) * (scale * share_of)
+    marks[0] = q_marks
+    marks[1] = k_marks
+    scores = packs.times(q_marks, k_marks, 1)
+    powers = jnp.exp(scores - packs.row_max(scores))
+    middle = powers / packs.row_sum(powers)
+    marks[2] = middle
+    col_sums = jnp.sum(middle, axis=0, keepdims=True)
+    col_top = packs.row_max(col_sums)
+    row_top = jnp.max(packs.row_sum(middle), axis=0, keepdims=True)
+    inverse_t = middle / (col_top * row_top)
+    product = packs.times(inverse_t, middle, 1)
+    for step in range(NEWTON):
+        second = packs.times(product, product)
+        pair = packs.times(cat([product, second], 0), second)
+        third, fourth = pair[:count], pair[count:]
+        for i, value in enumerate((product, second, third, inverse_t)):
+            chain[step, i] = value
+        blend = 0.25 * (13.0 * packs.unit - 15.0 * product + 7.0 * second - third)
+        product = 0.25 * (13.0 * product - 15.0 * second + 7.0 * third - fourth)
+        inverse_t = packs.times(blend, inverse_t)
+    marks[3] = inverse_t
+    def tall_scores(values, wide):
+        high, low = halves(values * scale)
+        both = mm(cat([packs.block(high), packs.block(low)], 0), wide, 1, 0)
+        return both[:head_width] + both[head_width:]
+
+    def per_head(value):
+        return value.reshape(nh, count, slot)
+
+    scores = per_head(tall_scores(k_marks, queries))
+    powers = jnp.exp(scores - jnp.max(scores, axis=1, keepdims=True))
+    first = (powers * (1.0 / jnp.sum(powers, axis=1, keepdims=True))).reshape(head_width, slot)
+    a1[...] = first
+    scores = jnp.where(live, tall_scores(q_marks, keys), -1e9)
+    powers = jnp.exp(scores - jnp.max(scores, axis=1, keepdims=True))
+    third = powers * (1.0 / jnp.sum(powers, axis=1, keepdims=True))
+    a3[...] = third
+    values = jnp.where(live, packed[2 * head_width :].astype(F32), 0.0).astype(BF16)
+    t_high, t_low = halves(third)
+    summary_t = packs.diagonal(mm(values, t_high, 1, 1) + mm(values, t_low, 1, 1))
+    weights_t = packs.times(summary_t, inverse_t)
+    marks[4] = summary_t
+    marks[5] = weights_t
+    w_high, w_low = halves(weights_t)
+    f_high, f_low = halves(first)
+    mixed = mm(cat([packs.block(w_high), packs.block(w_low)], 0), f_high, 1, 0)
+    mixed = mixed[:head_width] + mixed[head_width:] + mm(packs.block(w_high), f_low, 1, 0)
+    for h in range(nh):
+        part = slice(DIM * h, DIM * (h + 1))
+        conv = unwindow(mm(windows(values[part]), bands[0][h], 1, 1), DIM)
+        att[part] = jnp.where(live, mixed[part] + conv, 0.0).astype(BF16)
+    mine = pl.ds(pl.multiple_of(rows * me, rows), rows)
+    own_rows = pl.ds(pl.multiple_of(head_width * me, 64), head_width)
+    att_sent = []
+    for k in (2, 3, 1):
+        lanes = pl.ds(pl.multiple_of(rows * (me ^ k), rows), rows)
+        att_sent.append(send(att.at[:, lanes], heads.at[own_rows], (dp, me ^ k)))
+    heads[own_rows] = att[:, mine]
+    wout_fetch.wait()
+    tok_fetch.wait()
+    for copy in att_sent:
+        copy.wait()
+    heads_sent = send(heads, heads_x, mate)
+    branch = mm(heads[...], w_out[...], 0, 0)
+    normed, root_one = norm_forward(tok[...].astype(F32) + branch)
+    norm1_ref[...] = normed
+    first_norm = normed * gain_ref[0:1] + shift_ref[0:1]
+    first_ref[...] = first_norm
+    low = first_norm.astype(BF16)
+    low_t[...] = low.T
+    low_sent = send(low_t, low_x, mate)
+    wup_fetch.wait()
+    wdown_fetch.wait()
+    second_sum = None
+    act_sent = []
+    for i in range(quarters):
+        cols = slice(block * i, block * (i + 1))
+        active, slope_part = gelu_pair(mm(low, w_up[:, cols], 1, 0))
+        active = active.astype(BF16)
+        act[:rows, cols] = active
+        act_sent.append(send(act.at[:rows, cols], act.at[rows:, cols], mate))
+        slope[:, cols] = slope_part
+        part = mm(active, w_down[cols, :], 1, 0)
+        second_sum = part if second_sum is None else second_sum + part
+    normed_two, root_two = norm_forward(first_ref[...] + second_sum)
+    out_v[...] = (normed_two * gain_ref[1:2] + shift_ref[1:2]).astype(BF16)
+    stores = [fetch(out_v, out_hbm)]
+    grad_fetch.wait()
+    spot = me * rows + lax.broadcasted_iota(jnp.int32, (rows, 1), 0)
+    cotangent = jnp.where(spot < length, grad_in[...].astype(F32), 0.0)
+    sum_s[0] = jnp.zeros(sum_s.shape[1:], F32)
+    sum_s[0, 1:2] = jnp.sum(cotangent * normed_two, axis=0, keepdims=True)
+    sum_s[0, 3:4] = jnp.sum(cotangent, axis=0, keepdims=True)
+    g_two = norm_backward(cotangent, gain_ref[1:2], normed_two, root_two)
+    gr1_ref[...] = g_two
+    g_low = g_two.astype(BF16)
+    gst[...] = g_low.T
+    gst_sent = send(gst, gst_x, mate)
+    for copy in act_sent:
+        copy.wait()
+    gst_sent.wait()
+    lead = cat(
+        [
+            cat(
+                [
+                    ref[pl.ds(pl.multiple_of(head_width * (2 * x + core), 64), head_width), :]
+                    for ref in (gst, gst_x)
+                ],
+                1,
+            )
+            for x in range(2)
+        ],
+        0,
+    )
+    for pair in range(4):
+        total = mm(lead, act[:, 2 * down_cols * pair : 2 * down_cols * (pair + 1)], 1, 0)
+        total = total.astype(BF16)
+        for x in range(2):
+            for inner in range(2):
+                at = {"x": x, "y": inner, "l": pair % 2, "h": pair // 2}
+                for q in range(3):
+                    top = head_width * x + 64 * q
+                    acc_down[q, position(DOWN_ORDERS[q], at)] = total[
+                        top : top + 64, down_cols * inner : down_cols * (inner + 1)
+                    ]
+    downs = [spread(acc_down.at[q], got_down.at[q], DOWN_ORDERS[q]) for q in range(3)]
+    for chunk in downs:
+        chunk.start()
+    g_first = gr1_ref[...]
+    gh_sent = []
+    for i in range(quarters):
+        cols = slice(block * i, block * (i + 1))
+        part = (slope[:, cols] * mm(g_low, w_down[cols, :], 1, 1)).astype(BF16)
+        gh[:, cols] = part
+        g_first = g_first + mm(part, w_up[:, cols], 1, 1)
+        if i % 2:
+            lanes = pl.ds(pl.multiple_of(block * (i - core), 128), block)
+            gh_sent.append(send(gh.at[:, lanes], gh_x.at[i // 2], mate))
+    normed = norm1_ref[...]
+    sum_s[0, 0:1] = jnp.sum(g_first * normed, axis=0, keepdims=True)
+    sum_s[0, 2:3] = jnp.sum(g_first, axis=0, keepdims=True)
+    g_one = norm_backward(g_first, gain_ref[0:1], normed, root_one)
+    gr1_ref[...] = g_one
+    g_branch = g_one.astype(BF16)
+    gb[...] = g_branch
+    gatt[...] = mm(w_out[...], g_branch, 1, 1).astype(BF16)
+    g_sent = []
+    for k in (2, 3, 1):
+        src = gatt.at[pl.ds(pl.multiple_of(head_width * (me ^ k), 64), head_width)]
+        g_sent.append(send(src, g_in.at[:, mine], (dp, me ^ k)))
+    gb_sent = send(gb, gb_x, mate)
+    g_in[:, mine] = gatt[own_rows]
+    low_sent.wait()
+    for copy in gh_sent:
+        copy.wait()
+    lead = cat([low_t[...], low_x[...]], 1)
+    ups = [spread(acc_up.at[q], got_up.at[q], UP_ORDERS[q]) for q in range(3)]
+    for q in range(3):
+        for x in range(2):
+            lanes = pl.ds(pl.multiple_of(block * (2 * x + core) + 256 * q, 128), 256)
+            side = cat([gh[:, lanes], gh_x[x, :, 256 * q : 256 * (q + 1)]], 0)
+            total = mm(lead, side, 1, 0).astype(BF16)
+            for d in range(8):
+                at = {"x": x, "y": d % 2, "l": d // 2 % 2, "h": d // 4}
+                acc_up[q, position(UP_ORDERS[q], at)] = total[
+                    band_rows * d : band_rows * (d + 1)
+                ]
+        ups[q].start()
+    for chunk in downs:
+        chunk.step()
+    heads_sent.wait()
+    gb_sent.wait()
+    lead = cat([heads[...], heads_x[...]], 1)
+    both = cat([gb[...], gb_x[...]], 0)
+    band_half = band_rows // 2
+
+    def folded(total, d):
+        top = band_rows * d
+        return cat([total[top : top + band_half], total[top + band_half : top + band_rows]], 1)
+
+    for x in range(2):
+        left_cols = both[:, 2 * head_width * x : 2 * head_width * x + head_width]
+        right_cols = both[:, 2 * head_width * x + head_width : 2 * head_width * (x + 1)]
+        total = mm(lead, jnp.where(core == 0, left_cols, right_cols), 1, 0).astype(BF16)
+        for d in range(8):
+            at = {"x": x, "y": d % 2, "l": d // 2 % 2, "h": d // 4}
+            acc_out[position(OUT_ORDER, at)] = folded(total, d)
+    outs = spread(acc_out, got_out, OUT_ORDER)
+    outs.start()
+    tokens_t = everyone[...].reshape(slot, width).T
+    for copy in g_sent:
+        copy.wait()
+    grad = jnp.where(live, g_in[...].astype(F32), 0.0).astype(BF16)
+    values = jnp.where(live, packed[2 * head_width :].astype(F32), 0.0).astype(BF16)
+    first, third = a1[...], a3[...]
+    inverse_t, summary_t, weights_t = marks[3], marks[4], marks[5]
+    f_high, f_low = halves(first)
+    t_high, t_low = halves(third)
+    g_weights = packs.diagonal(mm(f_high, grad, 1, 1) + mm(f_low, grad, 1, 1))
+    g_summary = packs.times(inverse_t, g_weights)
+    s_high, s_low = halves(g_summary)
+    g_values = mm(packs.block(s_high), t_high, 0, 0) + mm(packs.block(s_low), t_high, 0, 0)
+    g_values = g_values + mm(packs.block(s_high), t_low, 0, 0)
+    flip_rows = lax.broadcasted_iota(jnp.int32, (128, 128), 0)
+    flip_cols = lax.broadcasted_iota(jnp.int32, (128, 128), 1)
+    flip = (flip_rows + flip_cols == 127).astype(F32).astype(BF16)
+    for h in range(nh):
+        part = slice(DIM * h, DIM * (h + 1))
+        g_wide = windows(grad[part])
+        total = g_values[part] + unwindow(mm(g_wide, bands[1][h], 1, 1), DIM)
+        gproj[2 * head_width + DIM * h : 2 * head_width + DIM * (h + 1)] = jnp.where(
+            live, total, 0.0
+        ).astype(BF16)
+        turned = mm(g_wide[:, 128:256], flip, 1, 0).astype(BF16)
+        gram = mm(turned, windows(values[part]), 0, 0)
+        gram = pltpu.roll(gram, 384 - 127, 1, stride=1, stride_axis=0)
+        found = pltpu.roll(jnp.sum(gram, axis=0, keepdims=True), 384 - 112, 1)
+        at = lax.broadcasted_iota(jnp.int32, found.shape, 1)
+        sum_s[0, pl.ds(4 + nh * me + h, 1), 0:384] = jnp.where(at < TAPS, found, 0.0)
+    p_sent = []
+
+    def share(part):
+        own = gproj.at[head_width * part : head_width * (part + 1)]
+        dst = pl.ds(pl.multiple_of(width * part + head_width * me, 64), head_width)
+        for k in (2, 3, 1):
+            lanes = pl.ds(pl.multiple_of(rows * (me ^ k), rows), rows)
+            p_sent.append(send(own.at[:, lanes], gp_in.at[dst], (dp, me ^ k)))
+        gp_in[dst] = own[:, mine]
+
+    projs = [spread(acc_qkv.at[j], got_qkv.at[j], QKV_ORDERS[j]) for j in range(3)]
+
+    def qkv_gradient(part):
+        total = mm(tokens_t, gproj[head_width * part : head_width * (part + 1)], 1, 1)
+        total = total.astype(BF16)
+        for d in range(8):
+            at = {"y": d % 2, "l": d // 2 % 2, "h": d // 4}
+            acc_qkv[part, position(QKV_ORDERS[part], at)] = folded(total, d)
+        projs[part].start()
+
+    share(2)
+    qkv_gradient(2)
+    sums = [mate] + [bits[name][1] for name in ("x", "y", "l", "h")]
+    sum_base = reserve(5)
+
+    def sum_start(k):
+        copy = copy_to(sum_s.at[k], sum_r.at[k], sems, sum_base + k, sums[k])
+        copy.start()
+        return copy
+
+    def sum_step(k, copy):
+        copy.wait()
+        total = sum_s[k] + sum_r[k]
+        if k == 4:
+            return total
+        sum_s[k + 1] = total
+        return sum_start(k + 1)
+
+    pending = sum_start(0)
+    outer = packs.times(g_weights, summary_t)
+    hold = jnp.zeros_like(outer)
+    for step in reversed(range(NEWTON)):
+        product, second, cube, inverse_t = [chain[step, i] for i in range(4)]
+        blend = 0.25 * (13.0 * packs.unit - 15.0 * product + 7.0 * second - cube)
+        inner = packs.times(inverse_t, outer)
+        by_inner = packs.times(cat([product, second], 0), inner)
+        zero_th, once, twice = inner, by_inner[:count], by_inner[count:]
+        if step < NEWTON - 1:
+            by_hold = packs.times(cat([product, second, cube], 0), hold)
+            zero_th = zero_th + by_hold[:count]
+            once = once + by_hold[count : 2 * count]
+            twice = twice + by_hold[2 * count :]
+        rest = packs.times(zero_th, 7.0 * product - second - 15.0 * packs.unit)
+        rest = rest + packs.times(once, 7.0 * packs.unit - product) - twice
+        pair = packs.times(cat([outer, hold], 0), blend)
+        outer, hold = pair[:count], pair[count:] + 0.25 * rest
+    w_high, w_low = halves(weights_t)
+    g_tall = mm(packs.block(w_high), grad, 0, 0) + mm(packs.block(w_low), grad, 0, 0)
+    along = jnp.sum(per_head(g_tall * first), axis=1, keepdims=True)
+    g_one = first * (per_head(g_tall) - along).reshape(head_width, slot)
+    g_tall = mm(cat([packs.block(s_high), packs.block(s_low)], 0), values, 1, 0)
+    g_tall = g_tall[:head_width] + g_tall[head_width:]
+    g_three = third * (g_tall - jnp.sum(g_tall * third, axis=1, keepdims=True))
+    queries = packed[:head_width]
+    keys = packed[head_width : 2 * head_width]
+
+    def tall_marks(high, low, wide):
+        both = mm(cat([high, low], 0), wide, 1, 1)
+        return packs.diagonal(both[:head_width] + both[head_width:]) * scale
+
+    one_high, one_low = halves(g_one)
+    three_high, three_low = halves(g_three)
+    g_k_marks = tall_marks(one_high, one_low, queries)
+    g_q_marks = tall_marks(three_high, three_low, keys)
+    q_marks, k_marks, middle = marks[0], marks[1], marks[2]
+    inverse_t = chain[0, 3]
+    col_sums = jnp.sum(middle, axis=0, keepdims=True)
+    row_sums = packs.row_sum(middle)
+    col_top = packs.row_max(col_sums)
+    row_top = jnp.max(row_sums, axis=0, keepdims=True)
+    norm = 1.0 / (col_top * row_top)
+    g_start_t = packs.turn(outer) + packs.times(packs.turn(hold), middle)
+    g_norm = -packs.row_sum(jnp.sum(g_start_t * inverse_t, axis=0, keepdims=True)) * norm
+    col_hit = (col_sums == col_top).astype(F32)
+    row_hit = (row_sums == row_top).astype(F32)
+    col_hit = col_hit / packs.row_sum(col_hit)
+    row_hit = row_hit / jnp.sum(row_hit, axis=0, keepdims=True)
+    g_middle = packs.times(hold, inverse_t) + g_start_t * norm
+    g_middle = g_middle + g_norm * (row_top * col_hit + col_top * row_hit)
+    g_two_s = middle * (g_middle - packs.row_sum(g_middle * middle))
+    g_q_marks = g_q_marks + packs.times(g_two_s, k_marks)
+    g_k_marks = g_k_marks + packs.times(packs.turn(g_two_s), q_marks)
+    for base, other, g_own, high in (
+        (0, k_marks, g_q_marks, one_high),
+        (head_width, q_marks, g_k_marks, three_high),
+    ):
+        m_high, m_low = halves(other)
+        l_high, l_low = halves(g_own * share_of)
+        total = mm(packs.block(m_high), high, 0, 0) + mm(packs.block(m_low), high, 0, 0)
+        total = total + mm(cat([l_high, l_low], 0), cat([member, member], 0), 0, 0)
+        gproj[base : base + head_width] = (total * scale).astype(BF16)
+    share(0)
+    share(1)
+    for chunk in downs:
+        chunk.step()
+    for chunk in ups:
+        chunk.step()
+    outs.step()
+    pending = sum_step(0, pending)
+    qkv_gradient(0)
+    qkv_gradient(1)
+    for chunk in downs:
+        chunk.step()
+    projs[2].step()
+    pending = sum_step(1, pending)
+    for chunk in ups:
+        chunk.step()
+    outs.step()
+    projs[0].step()
+    projs[1].step()
+    projs[2].step()
+    pending = sum_step(2, pending)
+    for q in range(3):
+        gdown_v[:, 64 * q : 64 * (q + 1)] = downs[q].finish().T
+    stores.append(fetch(gdown_v, gdown_hbm))
+    for copy in p_sent:
+        copy.wait()
+    in_v[...] = (gr1_ref[...] + mm(gp_in[...], w_qkv[...], 0, 1)).astype(BF16)
+    stores.append(fetch(in_v, in_hbm))
+    projs[0].step()
+    projs[1].step()
+    pending = sum_step(3, pending)
+    for chunk in ups:
+        chunk.step()
+    outs.step()
+    last = reserve(3)
+    for part in (2, 0, 1):
+        total = projs[part].finish()
+        goal = quarters * part + me
+        dest, where = lax.div(goal, 3), lax.rem(goal, 3)
+
+        @pl.when(dest == me)
+        def _():
+            slots[where] = total
+
+        @pl.when(dest != me)
+        def _():
+            fin[part] = total
+            pltpu.make_async_remote_copy(
+                src_ref=fin.at[part], dst_ref=slots.at[where],
+                send_sem=sems.at[0, last + part], recv_sem=sems.at[1, last + where],
+                device_id=(dp, dest), device_id_type=MESH,
+            ).start()
+
+    for q in range(3):
+        gup_v[:, 256 * q : 256 * (q + 1)] = ups[q].finish()
+    stores.append(fetch(gup_v, gup_hbm))
+    total = outs.finish()
+    gout_v[:band_half] = total[:, :head_width]
+    gout_v[band_half:] = total[:, head_width:]
+    stores.append(fetch(gout_v, gout_hbm))
+    total = sum_step(4, pending)
+    ggain_v[...] = total[0:2]
+    gshift_v[...] = total[2:4]
+    gtaps_v[...] = total[4:16, :TAPS]
+    stores.append(fetch(ggain_v, ggain_hbm))
+    stores.append(fetch(gshift_v, gshift_hbm))
+    stores.append(fetch(gtaps_v, gtaps_hbm))
+    for index in range(3):
+        goal = quarters * index + me
+        source = lax.rem(3 * me + index, quarters)
+
+        @pl.when(lax.div(goal, 3) != me)
+        def _():
+            copy_to(fin.at[index], slots.at[0], sems, last + index, mate).wait_send()
+
+        @pl.when(source != me)
+        def _():
+            copy_to(fin.at[0], slots.at[index], sems, last + index, mate).wait_recv()
+
+    for index in range(3):
+        got = slots[index]
+        cols = slice(head_width * index, head_width * (index + 1))
+        gqkv_v[:band_half, cols] = got[:, :head_width]
+        gqkv_v[band_half:, cols] = got[:, head_width:]
+    stores.append(fetch(gqkv_v, gqkv_hbm))
+    for copy in stores:
+        copy.wait()
+
+
+def final_kernel(*refs):
+    sem = refs[-1]
+    count = (len(refs) - 1) // 3
+    inward = [
+        pltpu.make_async_copy(refs[i], refs[2 * count + i], sem.at[0, i]) for i in range(count)
+    ]
+    outward = [
+        pltpu.make_async_copy(refs[2 * count + i], refs[count + i], sem.at[1, i])
+        for i in range(count)
+    ]
+    for copy in inward:
+        copy.start()
+    for got, put in zip(inward, outward):
+        got.wait()
+        put.start()
+    for copy in outward:
+        copy.wait()
+
+
+def per_device_fast(
+    tokens, w_qkv, w_out, w_up, w_down, norm_gains, norm_shifts, conv_kernels, seq_lengths,
+    seg_bounds, out_grad,
+):
+    rows, width = tokens.shape
+    ff = w_up.shape[1]
+    head_width = width // 4
+    slot = 4 * rows
+    band, down_cols = width // 8, ff // 8
+    whole = pl.BlockSpec(memory_space=VMEM)
+    anywhere = pl.BlockSpec(memory_space=pl.ANY)
+    shape = jax.ShapeDtypeStruct
+    outs = (
+        shape((rows, width), BF16),
+        shape((rows, width), BF16),
+        shape((band, w_qkv.shape[1] // 4), F32),
+        shape((band, width // 4), F32),
+        shape((band, ff // 4), F32),
+        shape((down_cols, width // 4), F32),
+        shape(norm_gains.shape, F32),
+        shape(norm_shifts.shape, F32),
+        shape(conv_kernels.shape, F32),
+    )
+    found = pl.pallas_call(
+        main_kernel,
+        out_shape=outs,
+        in_specs=[anywhere] * 6
+        + [whole] * 3
+        + [pl.BlockSpec(memory_space=pltpu.SMEM), whole],
+        out_specs=[anywhere] * 9,
+        scratch_shapes=[
+            VMEM((rows, width), BF16), VMEM((rows, width), BF16),
+            VMEM(w_qkv.shape, BF16), VMEM(w_out.shape, BF16),
+            VMEM(w_up.shape, BF16), VMEM(w_down.shape, BF16),
+            pltpu.SemaphoreType.DMA((32,)), pltpu.SemaphoreType.DMA((2, 120)),
+            VMEM((4, rows, width), BF16),
+            VMEM((3, 256, width), BF16),
+            VMEM((2, conv_kernels.shape[0], 384), F32),
+            VMEM((3 * head_width, slot), BF16),
+            VMEM((head_width, slot), F32), VMEM((head_width, slot), F32),
+            VMEM((NEWTON, 4, DIM, head_width), F32),
+            VMEM((6, DIM, head_width), F32),
+            VMEM((head_width, slot), BF16),
+            VMEM((width, rows), BF16), VMEM((width, rows), BF16),
+            VMEM((width, rows), BF16), VMEM((width, rows), BF16),
+            VMEM((2 * rows, ff), BF16),
+            VMEM((width, rows), BF16), VMEM((width, rows), BF16),
+            VMEM((rows, ff), F32),
+            VMEM((rows, ff), BF16), VMEM((2, rows, ff // 4), BF16),
+            VMEM((rows, width), BF16), VMEM((rows, width), BF16),
+            VMEM((width, rows), BF16),
+            VMEM((head_width, slot), BF16),
+            VMEM((3 * head_width, slot), BF16),
+            VMEM((3 * width, rows), BF16),
+            VMEM((rows, width), F32), VMEM((rows, width), F32), VMEM((rows, width), F32),
+            VMEM((5, 16, width), F32), VMEM((5, 16, width), F32),
+            VMEM((3, band // 2, 2 * head_width), F32),
+            VMEM((3, band // 2, 2 * head_width), F32),
+            VMEM((3, 16, 64, down_cols), BF16), VMEM((3, 15, 64, down_cols), BF16),
+            VMEM((3, 16, band, 256), BF16), VMEM((3, 15, band, 256), BF16),
+            VMEM((16, band // 2, 2 * head_width), BF16),
+            VMEM((15, band // 2, 2 * head_width), BF16),
+            VMEM((3, 8, band // 2, 2 * head_width), BF16),
+            VMEM((3, 7, band // 2, 2 * head_width), BF16),
+        ]
+        + [VMEM(out.shape, out.dtype) for out in outs],
+        compiler_params=pltpu.CompilerParams(
+            collective_id=0, has_side_effects=True, vmem_limit_bytes=63 * 2**20
+        ),
+        name="main_kernel",
+    )(
+        tokens, out_grad, w_qkv, w_out, w_up, w_down, norm_gains, norm_shifts, conv_kernels,
+        seq_lengths, seg_bounds,
+    )
+    return pl.pallas_call(
+        final_kernel,
+        out_shape=outs,
+        in_specs=[anywhere] * 9,
+        out_specs=[anywhere] * 9,
+        scratch_shapes=[VMEM(out.shape, out.dtype) for out in outs]
+        + [pltpu.SemaphoreType.DMA((2, 9))],
+        name="final_kernel",
+    )(*found)
 
 
 highest = lax.Precision.HIGHEST
@@ -243,8 +1060,9 @@
         P("dp", None),
         P(("dp", "head"), None),
     )
+    aligned = mesh.shape["dp"] == 8 and mesh.shape["head"] == 4
     return jax.shard_map(
-        per_device,
+        per_device_fast if aligned else per_device,
         mesh=mesh,
         in_specs=placed,
         out_specs=(

time: 718 us -> 114 us (0.16); the launches traced: 708 us -> 114 us
  waiting for transfers between devices: 296 us -> 0 us
  local copies, waits for them, and re-layouts: 138 us -> 1.86 us
  Pallas kernels: 0 us -> 111 us
  matrix products: 103 us -> 0 us
  blocking collectives: 73.4 us -> 0 us
  other arithmetic: 66.2 us -> 0 us
  between operations: 18.1 us -> 1.31 us
  starting transfers between devices: 12.7 us -> 0 us
    reduce_scatter x4 -> x0, waiting for transfers between devices: 280 us -> none  [the longest x1 141 us: per_device(): lax.psum_scatter(blocked_down, ('dp', 'head'), scatter_dimension=0, tiled...]
    pallas_call x0 -> x2, Pallas kernels: none -> 111 us  [the longest x1 108 us: per_device_fast(): pl.pallas_call(main_kernel, out_shape=outs, in_specs=[anywhere] * 6 + [wh...]
    dot_general x106 -> x0, matrix products: 103 us -> none  [the longest x4 18.4 us: row_contract(): lax.dot_general(left, right, (((0,), (0,)), ((), ())), preferred_element_...]
    psum x1 -> x0, blocking collectives: 41.2 us -> none  [per_device(): lax.psum((jnp.stack([grad_gain_one, grad_gain_two]), jnp.stack([grad_shif...]
    reshape x8 -> x0, local copies, waits for them, and re-layouts: 38 us -> none  [the longest x2 23.3 us: to_blocks(): matrix.reshape(dp_count, total_rows // dp_count, quarters, total_cols //...]
    all_to_all x1 -> x0, blocking collectives: 32.3 us -> none  [per_device(): lax.all_to_all(grad_packed_low, 'head', split_axis=0, concat_axis=2, tile...]
    transpose x3 -> x0, local copies, waits for them, and re-layouts: 30.9 us -> none  [to_blocks(): shaped.transpose(0, 2, 1, 3)]
    reduce_sum x11 -> x0, other arithmetic: 29.8 us -> none  [the longest x2 21.9 us: shifted_conv(): total = total + kernel[offset] * padded[offset:offset + slot_len]]
  transfers between devices with their start and end apart: 7 -> 0, of which waited for: 5 -> 0; matrix products, arithmetic and copies ran while one was open for 28% -> 0% of each run, Pallas kernels for 0% -> 0%
where the time goes in v2:
time: 114 us
  Pallas kernels  111 us (97%)
  local copies, waits for them, and re-layouts  1.86 us (2%)
  between operations  1.31 us (1%)
    pallas_call x1, Pallas kernels, per_device_fast(): pl.pallas_call(main_kernel, out_shape=outs, in_specs=[anywhere] * 6 + [wh...  108 us
    pallas_call x1, Pallas kernels, per_device_fast(): pl.pallas_call(final_kernel, out_shape=outs, in_specs=[anywhere] * 9, out...  2.4 us

profile of v2, /device:TPU:0, one launch (start us, length us, event | category | flops | bytes accessed | tf_op | source)
XLA Modules:
  0.0 113.7 jit_solution(16470698776970610777)
XLA Ops:
  1.3 108.1 %main_kernel.1 = (bf16[256,768]{1,0:T(8,128)(2,1)}, bf16[256,768]{1,0:T(8,128)(2,1)}, f32[96,576]{1,0:T(8,128)}, f32[96,192]{1,0:T(8,128)}, f32[96,768]{1,0:T(8,...) custom-call(bf16[256,768]{1,0:T(8,128)(2,1)} %tok_hbm.1, ...), custom_call_target="tpu_custom_call" | custom-call | tf_op jit(solution)/shard_map/main_kernel/pallas_call | solution.py:764
  109.4 2.4 %final_kernel.1 = (bf16[256,768]{1,0:T(8,128)(2,1)}, bf16[256,768]{1,0:T(8,128)(2,1)}, f32[96,576]{1,0:T(8,128)}, f32[96,192]{1,0:T(8,128)}, f32[96,768]{1,0:T(8...) custom-call(bf16[256,768]{1,0:T(8,128)(2,1)} %get-tuple-element.18.refs_0_, ...), custom_call_target="tpu_custom_call" | custom-call | tf_op jit(solution)/shard_map/final_kernel/pallas_call | solution.py:815
  111.9 1.9 %copy.20 = f32[384,192]{0,1:T(8,128)} copy(f32[384,192]{1,0:T(8,128)} %get-tuple-element.32) | data formatting | bytes 589824 | tf_op jit(solution)/shard_map/final_kernel/pallas_call | solution.py:815

commit v3 on v2

--- a/solution.py
+++ b/solution.py
@@ -190,10 +190,18 @@
     return spot
 
 
-DOWN_ORDERS = (("x", "y", "l", "h"), ("y", "l", "x", "h"), ("l", "y", "x", "h"))
-UP_ORDERS = (("y", "l", "x", "h"), ("l", "y", "x", "h"), ("x", "l", "y", "h"))
-OUT_ORDER = ("y", "l", "x", "h")
-QKV_ORDERS = (("y", "l", "h"), ("l", "y", "h"), ("l", "y", "h"))
+DOWN_ORDERS = ("lyxh", "yxlh", "xlyh")
+UP_ORDERS = ("ylxh", "xylh", "xylh")
+OUT_ORDER = "lyhx"
+SUM_ORDER = "chlxy"
+QKV_ORDERS = ("ylh", "ylh", "ylh")
+SCHEDULE = (
+    "DG", "FB", "UG0", "OG", "D0", "D1", "D2", "AV", "S0", "O", "QG2", "S1", "NB1", "U0",
+    "D1", "UG1", "NB2", "D2", "UG2", "SM", "S2", "D0", "MM", "O", "QG0", "U0", "QG1", "D1",
+    "P2", "S3", "D2", "U1", "O", "P0", "D1", "P2", "P1", "D2", "U2", "P0", "U1", "P2", "D0",
+    "P1", "P0", "U2", "U1", "D0", "IN", "P1", "U0", "U2", "S4", "O", "U1", "S5", "U0", "U2",
+    "GQ",
+)
 
 
 def main_kernel(
@@ -252,10 +260,6 @@
     own_fetch = fetch(tok_hbm, everyone.at[me])
     tok_fetch = fetch(tok_hbm, tok)
     wqkv_fetch = fetch(wqkv_hbm, w_qkv)
-    wout_fetch = fetch(wout_hbm, w_out)
-    wup_fetch = fetch(wup_hbm, w_up)
-    wdown_fetch = fetch(wdown_hbm, w_down)
-    grad_fetch = fetch(grad_hbm, grad_in)
     greet([(dp, me ^ k) for k in (1, 2, 3)] + [(dp ^ k, me) for k in (1, 2, 4)])
     half = rows // 2
     far = []
@@ -264,6 +268,10 @@
         far.append(send(tok_hbm.at[part], everyone.at[me, part], (dp, me ^ 2)))
     near = send(tok_hbm, everyone.at[me], mate)
     wqkv_fetch.wait()
+    wout_fetch = fetch(wout_hbm, w_out)
+    wup_fetch = fetch(wup_hbm, w_up)
+    wdown_fetch = fetch(wdown_hbm, w_down)
+    grad_fetch = fetch(grad_hbm, grad_in)
     odd = lax.rem(me, 2)
     for part in range(3):
         start = pl.multiple_of(part * width + 2 * head_width * lax.div(me, 2) + 128 * odd, 128)
@@ -411,125 +419,94 @@
     for copy in act_sent:
         copy.wait()
     gst_sent.wait()
-    lead = cat(
-        [
-            cat(
-                [
-                    ref[pl.ds(pl.multiple_of(head_width * (2 * x + core), 64), head_width), :]
-                    for ref in (gst, gst_x)
-                ],
-                1,
-            )
-            for x in range(2)
-        ],
-        0,
-    )
-    for pair in range(4):
-        total = mm(lead, act[:, 2 * down_cols * pair : 2 * down_cols * (pair + 1)], 1, 0)
-        total = total.astype(BF16)
-        for x in range(2):
-            for inner in range(2):
-                at = {"x": x, "y": inner, "l": pair % 2, "h": pair // 2}
-                for q in range(3):
-                    top = head_width * x + 64 * q
-                    acc_down[q, position(DOWN_ORDERS[q], at)] = total[
-                        top : top + 64, down_cols * inner : down_cols * (inner + 1)
-                    ]
+    s = {}
     downs = [spread(acc_down.at[q], got_down.at[q], DOWN_ORDERS[q]) for q in range(3)]
-    for chunk in downs:
-        chunk.start()
-    g_first = gr1_ref[...]
-    gh_sent = []
-    for i in range(quarters):
-        cols = slice(block * i, block * (i + 1))
-        part = (slope[:, cols] * mm(g_low, w_down[cols, :], 1, 1)).astype(BF16)
-        gh[:, cols] = part
-        g_first = g_first + mm(part, w_up[:, cols], 1, 1)
-        if i % 2:
-            lanes = pl.ds(pl.multiple_of(block * (i - core), 128), block)
-            gh_sent.append(send(gh.at[:, lanes], gh_x.at[i // 2], mate))
-    normed = norm1_ref[...]
-    sum_s[0, 0:1] = jnp.sum(g_first * normed, axis=0, keepdims=True)
-    sum_s[0, 2:3] = jnp.sum(g_first, axis=0, keepdims=True)
-    g_one = norm_backward(g_first, gain_ref[0:1], normed, root_one)
-    gr1_ref[...] = g_one
-    g_branch = g_one.astype(BF16)
-    gb[...] = g_branch
-    gatt[...] = mm(w_out[...], g_branch, 1, 1).astype(BF16)
-    g_sent = []
-    for k in (2, 3, 1):
-        src = gatt.at[pl.ds(pl.multiple_of(head_width * (me ^ k), 64), head_width)]
-        g_sent.append(send(src, g_in.at[:, mine], (dp, me ^ k)))
-    gb_sent = send(gb, gb_x, mate)
-    g_in[:, mine] = gatt[own_rows]
-    low_sent.wait()
-    for copy in gh_sent:
-        copy.wait()
-    lead = cat([low_t[...], low_x[...]], 1)
     ups = [spread(acc_up.at[q], got_up.at[q], UP_ORDERS[q]) for q in range(3)]
-    for q in range(3):
+    outs = spread(acc_out, got_out, OUT_ORDER)
+    projs = [spread(acc_qkv.at[j], got_qkv.at[j], QKV_ORDERS[j]) for j in range(3)]
+    sum_base = reserve(5)
+    last = reserve(3)
+    band_half = band_rows // 2
+    p_sent = []
+
+    def folded(total, d):
+        top = band_rows * d
+        return cat([total[top : top + band_half], total[top + band_half : top + band_rows]], 1)
+
+    def places(x, d):
+        return {"x": x, "y": d % 2, "l": d // 2 % 2, "h": d // 4}
+
+    def down_gradient():
+        tops = [pl.ds(pl.multiple_of(head_width * (2 * x + core), 64), head_width) for x in (0, 1)]
+        lead = cat([cat([gst[top, :], gst_x[top, :]], 1) for top in tops], 0)
+        for pair in range(4):
+            total = mm(lead, act[:, 2 * down_cols * pair : 2 * down_cols * (pair + 1)], 1, 0)
+            total = total.astype(BF16)
+            for x in range(2):
+                for inner in range(2):
+                    at = places(x, 2 * pair + inner)
+                    for q in range(3):
+                        top = head_width * x + 64 * q
+                        acc_down[q, position(DOWN_ORDERS[q], at)] = total[
+                            top : top + 64, down_cols * inner : down_cols * (inner + 1)
+                        ]
+        for chunk in downs:
+            chunk.start()
+
+    def forward_back():
+        g_first = gr1_ref[...]
+        s["gh"] = []
+        for i in range(quarters):
+            cols = slice(block * i, block * (i + 1))
+            part = (slope[:, cols] * mm(g_low, w_down[cols, :], 1, 1)).astype(BF16)
+            gh[:, cols] = part
+            g_first = g_first + mm(part, w_up[:, cols], 1, 1)
+            if i % 2:
+                lanes = pl.ds(pl.multiple_of(block * (i - core), 128), block)
+                s["gh"].append(send(gh.at[:, lanes], gh_x.at[i // 2], mate))
+        normed = norm1_ref[...]
+        sum_s[0, 0:1] = jnp.sum(g_first * normed, axis=0, keepdims=True)
+        sum_s[0, 2:3] = jnp.sum(g_first, axis=0, keepdims=True)
+        g_one = norm_backward(g_first, gain_ref[0:1], normed, root_one)
+        gr1_ref[...] = g_one
+        g_branch = g_one.astype(BF16)
+        gb[...] = g_branch
+        gatt[...] = mm(w_out[...], g_branch, 1, 1).astype(BF16)
+        s["g"] = []
+        for k in (2, 3, 1):
+            src = gatt.at[pl.ds(pl.multiple_of(head_width * (me ^ k), 64), head_width)]
+            s["g"].append(send(src, g_in.at[:, mine], (dp, me ^ k)))
+        s["gb"] = send(gb, gb_x, mate)
+        g_in[:, mine] = gatt[own_rows]
+
+    def up_gradient(q):
+        if q == 0:
+            low_sent.wait()
+            for copy in s["gh"]:
+                copy.wait()
+            s["lead"] = cat([low_t[...], low_x[...]], 1)
         for x in range(2):
             lanes = pl.ds(pl.multiple_of(block * (2 * x + core) + 256 * q, 128), 256)
             side = cat([gh[:, lanes], gh_x[x, :, 256 * q : 256 * (q + 1)]], 0)
-            total = mm(lead, side, 1, 0).astype(BF16)
+            total = mm(s["lead"], side, 1, 0).astype(BF16)
             for d in range(8):
-                at = {"x": x, "y": d % 2, "l": d // 2 % 2, "h": d // 4}
-                acc_up[q, position(UP_ORDERS[q], at)] = total[
+                acc_up[q, position(UP_ORDERS[q], places(x, d))] = total[
                     band_rows * d : band_rows * (d + 1)
                 ]
         ups[q].start()
-    for chunk in downs:
-        chunk.step()
-    heads_sent.wait()
-    gb_sent.wait()
-    lead = cat([heads[...], heads_x[...]], 1)
-    both = cat([gb[...], gb_x[...]], 0)
-    band_half = band_rows // 2
-
-    def folded(total, d):
-        top = band_rows * d
-        return cat([total[top : top + band_half], total[top + band_half : top + band_rows]], 1)
-
-    for x in range(2):
-        left_cols = both[:, 2 * head_width * x : 2 * head_width * x + head_width]
-        right_cols = both[:, 2 * head_width * x + head_width : 2 * head_width * (x + 1)]
-        total = mm(lead, jnp.where(core == 0, left_cols, right_cols), 1, 0).astype(BF16)
-        for d in range(8):
-            at = {"x": x, "y": d % 2, "l": d // 2 % 2, "h": d // 4}
-            acc_out[position(OUT_ORDER, at)] = folded(total, d)
-    outs = spread(acc_out, got_out, OUT_ORDER)
-    outs.start()
-    tokens_t = everyone[...].reshape(slot, width).T
-    for copy in g_sent:
-        copy.wait()
-    grad = jnp.where(live, g_in[...].astype(F32), 0.0).astype(BF16)
-    values = jnp.where(live, packed[2 * head_width :].astype(F32), 0.0).astype(BF16)
-    first, third = a1[...], a3[...]
-    inverse_t, summary_t, weights_t = marks[3], marks[4], marks[5]
-    f_high, f_low = halves(first)
-    t_high, t_low = halves(third)
-    g_weights = packs.diagonal(mm(f_high, grad, 1, 1) + mm(f_low, grad, 1, 1))
-    g_summary = packs.times(inverse_t, g_weights)
-    s_high, s_low = halves(g_summary)
-    g_values = mm(packs.block(s_high), t_high, 0, 0) + mm(packs.block(s_low), t_high, 0, 0)
-    g_values = g_values + mm(packs.block(s_high), t_low, 0, 0)
-    flip_rows = lax.broadcasted_iota(jnp.int32, (128, 128), 0)
-    flip_cols = lax.broadcasted_iota(jnp.int32, (128, 128), 1)
-    flip = (flip_rows + flip_cols == 127).astype(F32).astype(BF16)
-    for h in range(nh):
-        part = slice(DIM * h, DIM * (h + 1))
-        g_wide = windows(grad[part])
-        total = g_values[part] + unwindow(mm(g_wide, bands[1][h], 1, 1), DIM)
-        gproj[2 * head_width + DIM * h : 2 * head_width + DIM * (h + 1)] = jnp.where(
-            live, total, 0.0
-        ).astype(BF16)
-        turned = mm(g_wide[:, 128:256], flip, 1, 0).astype(BF16)
-        gram = mm(turned, windows(values[part]), 0, 0)
-        gram = pltpu.roll(gram, 384 - 127, 1, stride=1, stride_axis=0)
-        found = pltpu.roll(jnp.sum(gram, axis=0, keepdims=True), 384 - 112, 1)
-        at = lax.broadcasted_iota(jnp.int32, found.shape, 1)
-        sum_s[0, pl.ds(4 + nh * me + h, 1), 0:384] = jnp.where(at < TAPS, found, 0.0)
-    p_sent = []
+
+    def out_gradient():
+        heads_sent.wait()
+        s["gb"].wait()
+        lead = cat([heads[...], heads_x[...]], 1)
+        both = cat([gb[...], gb_x[...]], 0)
+        for x in range(2):
+            left_cols = both[:, 2 * head_width * x : 2 * head_width * x + head_width]
+            right_cols = both[:, 2 * head_width * x + head_width : 2 * head_width * (x + 1)]
+            total = mm(lead, jnp.where(core == 0, left_cols, right_cols), 1, 0).astype(BF16)
+            for d in range(8):
+                acc_out[position(OUT_ORDER, places(x, d))] = folded(total, d)
+        outs.start()
 
     def share(part):
         own = gproj.at[head_width * part : head_width * (part + 1)]
@@ -539,133 +516,164 @@
             p_sent.append(send(own.at[:, lanes], gp_in.at[dst], (dp, me ^ k)))
         gp_in[dst] = own[:, mine]
 
-    projs = [spread(acc_qkv.at[j], got_qkv.at[j], QKV_ORDERS[j]) for j in range(3)]
+    def values_back():
+        s["tokens_t"] = everyone[...].reshape(slot, width).T
+        for copy in s["g"]:
+            copy.wait()
+        grad = jnp.where(live, g_in[...].astype(F32), 0.0).astype(BF16)
+        values = jnp.where(live, packed[2 * head_width :].astype(F32), 0.0).astype(BF16)
+        f_high, f_low = halves(a1[...])
+        t_high, t_low = halves(a3[...])
+        g_weights = packs.diagonal(mm(f_high, grad, 1, 1) + mm(f_low, grad, 1, 1))
+        s_high, s_low = halves(packs.times(marks[3], g_weights))
+        g_values = mm(packs.block(s_high), t_high, 0, 0) + mm(packs.block(s_low), t_high, 0, 0)
+        g_values = g_values + mm(packs.block(s_high), t_low, 0, 0)
+        flip_rows = lax.broadcasted_iota(jnp.int32, (128, 128), 0)
+        flip_cols = lax.broadcasted_iota(jnp.int32, (128, 128), 1)
+        flip = (flip_rows + flip_cols == 127).astype(F32).astype(BF16)
+        for h in range(nh):
+            part = slice(DIM * h, DIM * (h + 1))
+            g_wide = windows(grad[part])
+            total = g_values[part] + unwindow(mm(g_wide, bands[1][h], 1, 1), DIM)
+            gproj[2 * head_width + DIM * h : 2 * head_width + DIM * (h + 1)] = jnp.where(
+                live, total, 0.0
+            ).astype(BF16)
+            turned = mm(g_wide[:, 128:256], flip, 1, 0).astype(BF16)
+            gram = mm(turned, windows(values[part]), 0, 0)
+            gram = pltpu.roll(gram, 384 - 127, 1, stride=1, stride_axis=0)
+            found = pltpu.roll(jnp.sum(gram, axis=0, keepdims=True), 384 - 112, 1)
+            at = lax.broadcasted_iota(jnp.int32, (1, 128), 1)
+            lanes = pl.ds(pl.multiple_of(128 * me, 128), 128)
+            sum_s[0, 4 + h : 5 + h, lanes] = jnp.where(at < TAPS, found[:, :128], 0.0)
+        s.update(grad=grad, values=values, s_high=s_high, s_low=s_low)
+        s["outer"] = packs.times(g_weights, marks[4])
+        s["hold"] = jnp.zeros_like(s["outer"])
+        share(2)
 
     def qkv_gradient(part):
-        total = mm(tokens_t, gproj[head_width * part : head_width * (part + 1)], 1, 1)
+        total = mm(s["tokens_t"], gproj[head_width * part : head_width * (part + 1)], 1, 1)
         total = total.astype(BF16)
         for d in range(8):
-            at = {"y": d % 2, "l": d // 2 % 2, "h": d // 4}
-            acc_qkv[part, position(QKV_ORDERS[part], at)] = folded(total, d)
+            acc_qkv[part, position(QKV_ORDERS[part], places(0, d))] = folded(total, d)
         projs[part].start()
 
-    share(2)
-    qkv_gradient(2)
-    sums = [mate] + [bits[name][1] for name in ("x", "y", "l", "h")]
-    sum_base = reserve(5)
-
-    def sum_start(k):
-        copy = copy_to(sum_s.at[k], sum_r.at[k], sems, sum_base + k, sums[k])
-        copy.start()
-        return copy
-
-    def sum_step(k, copy):
-        copy.wait()
-        total = sum_s[k] + sum_r[k]
-        if k == 4:
-            return total
-        sum_s[k + 1] = total
-        return sum_start(k + 1)
-
-    pending = sum_start(0)
-    outer = packs.times(g_weights, summary_t)
-    hold = jnp.zeros_like(outer)
-    for step in reversed(range(NEWTON)):
-        product, second, cube, inverse_t = [chain[step, i] for i in range(4)]
-        blend = 0.25 * (13.0 * packs.unit - 15.0 * product + 7.0 * second - cube)
-        inner = packs.times(inverse_t, outer)
-        by_inner = packs.times(cat([product, second], 0), inner)
-        zero_th, once, twice = inner, by_inner[:count], by_inner[count:]
-        if step < NEWTON - 1:
-            by_hold = packs.times(cat([product, second, cube], 0), hold)
-            zero_th = zero_th + by_hold[:count]
-            once = once + by_hold[count : 2 * count]
-            twice = twice + by_hold[2 * count :]
-        rest = packs.times(zero_th, 7.0 * product - second - 15.0 * packs.unit)
-        rest = rest + packs.times(once, 7.0 * packs.unit - product) - twice
-        pair = packs.times(cat([outer, hold], 0), blend)
-        outer, hold = pair[:count], pair[count:] + 0.25 * rest
-    w_high, w_low = halves(weights_t)
-    g_tall = mm(packs.block(w_high), grad, 0, 0) + mm(packs.block(w_low), grad, 0, 0)
-    along = jnp.sum(per_head(g_tall * first), axis=1, keepdims=True)
-    g_one = first * (per_head(g_tall) - along).reshape(head_width, slot)
-    g_tall = mm(cat([packs.block(s_high), packs.block(s_low)], 0), values, 1, 0)
-    g_tall = g_tall[:head_width] + g_tall[head_width:]
-    g_three = third * (g_tall - jnp.sum(g_tall * third, axis=1, keepdims=True))
-    queries = packed[:head_width]
-    keys = packed[head_width : 2 * head_width]
-
-    def tall_marks(high, low, wide):
-        both = mm(cat([high, low], 0), wide, 1, 1)
-        return packs.diagonal(both[:head_width] + both[head_width:]) * scale
-
-    one_high, one_low = halves(g_one)
-    three_high, three_low = halves(g_three)
-    g_k_marks = tall_marks(one_high, one_low, queries)
-    g_q_marks = tall_marks(three_high, three_low, keys)
-    q_marks, k_marks, middle = marks[0], marks[1], marks[2]
-    inverse_t = chain[0, 3]
-    col_sums = jnp.sum(middle, axis=0, keepdims=True)
-    row_sums = packs.row_sum(middle)
-    col_top = packs.row_max(col_sums)
-    row_top = jnp.max(row_sums, axis=0, keepdims=True)
-    norm = 1.0 / (col_top * row_top)
-    g_start_t = packs.turn(outer) + packs.times(packs.turn(hold), middle)
-    g_norm = -packs.row_sum(jnp.sum(g_start_t * inverse_t, axis=0, keepdims=True)) * norm
-    col_hit = (col_sums == col_top).astype(F32)
-    row_hit = (row_sums == row_top).astype(F32)
-    col_hit = col_hit / packs.row_sum(col_hit)
-    row_hit = row_hit / jnp.sum(row_hit, axis=0, keepdims=True)
-    g_middle = packs.times(hold, inverse_t) + g_start_t * norm
-    g_middle = g_middle + g_norm * (row_top * col_hit + col_top * row_hit)
-    g_two_s = middle * (g_middle - packs.row_sum(g_middle * middle))
-    g_q_marks = g_q_marks + packs.times(g_two_s, k_marks)
-    g_k_marks = g_k_marks + packs.times(packs.turn(g_two_s), q_marks)
-    for base, other, g_own, high in (
-        (0, k_marks, g_q_marks, one_high),
-        (head_width, q_marks, g_k_marks, three_high),
-    ):
-        m_high, m_low = halves(other)
-        l_high, l_low = halves(g_own * share_of)
-        total = mm(packs.block(m_high), high, 0, 0) + mm(packs.block(m_low), high, 0, 0)
-        total = total + mm(cat([l_high, l_low], 0), cat([member, member], 0), 0, 0)
-        gproj[base : base + head_width] = (total * scale).astype(BF16)
-    share(0)
-    share(1)
-    for chunk in downs:
-        chunk.step()
-    for chunk in ups:
-        chunk.step()
-    outs.step()
-    pending = sum_step(0, pending)
-    qkv_gradient(0)
-    qkv_gradient(1)
-    for chunk in downs:
-        chunk.step()
-    projs[2].step()
-    pending = sum_step(1, pending)
-    for chunk in ups:
-        chunk.step()
-    outs.step()
-    projs[0].step()
-    projs[1].step()
-    projs[2].step()
-    pending = sum_step(2, pending)
-    for q in range(3):
-        gdown_v[:, 64 * q : 64 * (q + 1)] = downs[q].finish().T
-    stores.append(fetch(gdown_v, gdown_hbm))
-    for copy in p_sent:
-        copy.wait()
-    in_v[...] = (gr1_ref[...] + mm(gp_in[...], w_qkv[...], 0, 1)).astype(BF16)
-    stores.append(fetch(in_v, in_hbm))
-    projs[0].step()
-    projs[1].step()
-    pending = sum_step(3, pending)
-    for chunk in ups:
-        chunk.step()
-    outs.step()
-    last = reserve(3)
-    for part in (2, 0, 1):
+    sums = [mate if name == "c" else bits[name][1] for name in SUM_ORDER]
+
+    def sum_step(k):
+        if k:
+            s["sum"].wait()
+            total = sum_s[k - 1] + sum_r[k - 1]
+            if k == 5:
+                ggain_v[...] = total[0:2]
+                gshift_v[...] = total[2:4]
+                for n in range(gtaps_v.shape[0]):
+                    at = 128 * (n // nh)
+                    row = 4 + n % nh
+                    gtaps_v[n : n + 1] = total[row : row + 1, at : at + TAPS]
+                stores.append(fetch(ggain_v, ggain_hbm))
+                stores.append(fetch(gshift_v, gshift_hbm))
+                stores.append(fetch(gtaps_v, gtaps_hbm))
+                return
+            sum_s[k] = total
+        s["sum"] = copy_to(sum_s.at[k], sum_r.at[k], sems, sum_base + k, sums[k])
+        s["sum"].start()
+
+    def newton_back(steps):
+        outer, hold = s["outer"], s["hold"]
+        for step in steps:
+            product, second, cube, inverse_t = [chain[step, i] for i in range(4)]
+            blend = 0.25 * (13.0 * packs.unit - 15.0 * product + 7.0 * second - cube)
+            inner = packs.times(inverse_t, outer)
+            by_inner = packs.times(cat([product, second], 0), inner)
+            zero_th, once, twice = inner, by_inner[:count], by_inner[count:]
+            if step < NEWTON - 1:
+                by_hold = packs.times(cat([product, second, cube], 0), hold)
+                zero_th = zero_th + by_hold[:count]
+                once = once + by_hold[count : 2 * count]
+                twice = twice + by_hold[2 * count :]
+            rest = packs.times(zero_th, 7.0 * product - second - 15.0 * packs.unit)
+            rest = rest + packs.times(once, 7.0 * packs.unit - product) - twice
+            pair = packs.times(cat([outer, hold], 0), blend)
+            outer, hold = pair[:count], pair[count:] + 0.25 * rest
+        s["outer"], s["hold"] = outer, hold
+
+    def softmax_back():
+        first, third = a1[...], a3[...]
+        w_high, w_low = halves(marks[5])
+        g_tall = mm(packs.block(w_high), s["grad"], 0, 0) + mm(packs.block(w_low), s["grad"], 0, 0)
+        along = jnp.sum(per_head(g_tall * first), axis=1, keepdims=True)
+        g_one = first * (per_head(g_tall) - along).reshape(head_width, slot)
+        g_tall = mm(cat([packs.block(s["s_high"]), packs.block(s["s_low"])], 0), s["values"], 1, 0)
+        g_tall = g_tall[:head_width] + g_tall[head_width:]
+        g_three = third * (g_tall - jnp.sum(g_tall * third, axis=1, keepdims=True))
+
+        def tall_marks(high, low, wide):
+            both = mm(cat([high, low], 0), wide, 1, 1)
+            return packs.diagonal(both[:head_width] + both[head_width:]) * scale
+
+        one_high, one_low = halves(g_one)
+        three_high, three_low = halves(g_three)
+        s["g_k"] = tall_marks(one_high, one_low, packed[:head_width])
+        s["g_q"] = tall_marks(three_high, three_low, packed[head_width : 2 * head_width])
+        s["one"], s["three"] = one_high, three_high
+
+    def middle_back():
+        q_marks, k_marks, middle = marks[0], marks[1], marks[2]
+        outer, hold = s["outer"], s["hold"]
+        inverse_t = chain[0, 3]
+        col_sums = jnp.sum(middle, axis=0, keepdims=True)
+        row_sums = packs.row_sum(middle)
+        col_top = packs.row_max(col_sums)
+        row_top = jnp.max(row_sums, axis=0, keepdims=True)
+        norm = 1.0 / (col_top * row_top)
+        g_start_t = packs.turn(outer) + packs.times(packs.turn(hold), middle)
+        g_norm = -packs.row_sum(jnp.sum(g_start_t * inverse_t, axis=0, keepdims=True)) * norm
+        col_hit = (col_sums == col_top).astype(F32)
+        row_hit = (row_sums == row_top).astype(F32)
+        col_hit = col_hit / packs.row_sum(col_hit)
+        row_hit = row_hit / jnp.sum(row_hit, axis=0, keepdims=True)
+        g_middle = packs.times(hold, inverse_t) + g_start_t * norm
+        g_middle = g_middle + g_norm * (row_top * col_hit + col_top * row_hit)
+        g_two_s = middle * (g_middle - packs.row_sum(g_middle * middle))
+        g_q_marks = s["g_q"] + packs.times(g_two_s, k_marks)
+        g_k_marks = s["g_k"] + packs.times(packs.turn(g_two_s), q_marks)
+        for part, other, g_own, high in (
+            (0, k_marks, g_q_marks, s["one"]),
+            (1, q_marks, g_k_marks, s["three"]),
+        ):
+            m_high, m_low = halves(other)
+            l_high, l_low = halves(g_own * share_of)
+            total = mm(packs.block(m_high), high, 0, 0) + mm(packs.block(m_low), high, 0, 0)
+            total = total + mm(cat([l_high, l_low], 0), cat([member, member], 0), 0, 0)
+            gproj[head_width * part : head_width * (part + 1)] = (total * scale).astype(BF16)
+            share(part)
+
+    def input_gradient():
+        wqkv = w_qkv[...]
+        for copy in p_sent:
+            copy.wait()
+        in_v[...] = (gr1_ref[...] + mm(gp_in[...], wqkv, 0, 1)).astype(BF16)
+        stores.append(fetch(in_v, in_hbm))
+
+    def finish_down(q):
+        gdown_v[64 * q : 64 * (q + 1)] = downs[q].finish()
+        s["downs"] = s.get("downs", 0) + 1
+        if s["downs"] == 3:
+            stores.append(fetch(gdown_v, gdown_hbm))
+
+    def finish_up(q):
+        gup_v[:, 256 * q : 256 * (q + 1)] = ups[q].finish()
+        s["ups"] = s.get("ups", 0) + 1
+        if s["ups"] == 3:
+            stores.append(fetch(gup_v, gup_hbm))
+
+    def finish_out():
+        total = outs.finish()
+        gout_v[:band_half] = total[:, :head_width]
+        gout_v[band_half:] = total[:, head_width:]
+        stores.append(fetch(gout_v, gout_hbm))
+
+    def finish_proj(part):
         total = projs[part].finish()
         goal = quarters * part + me
         dest, where = lax.div(goal, 3), lax.rem(goal, 3)
@@ -683,38 +691,50 @@
                 device_id=(dp, dest), device_id_type=MESH,
             ).start()
 
+    def collect():
+        for index in range(3):
+            goal = quarters * index + me
+            source = lax.rem(3 * me + index, quarters)
+
+            @pl.when(lax.div(goal, 3) != me)
+            def _():
+                copy_to(fin.at[index], slots.at[0], sems, last + index, mate).wait_send()
+
+            @pl.when(source != me)
+            def _():
+                copy_to(fin.at[0], slots.at[index], sems, last + index, mate).wait_recv()
+
+        for index in range(3):
+            got = slots[index]
+            cols = slice(head_width * index, head_width * (index + 1))
+            gqkv_v[:band_half, cols] = got[:, :head_width]
+            gqkv_v[band_half:, cols] = got[:, head_width:]
+        stores.append(fetch(gqkv_v, gqkv_hbm))
+
+    table = {
+        "DG": down_gradient, "FB": forward_back, "OG": out_gradient, "AV": values_back,
+        "SM": softmax_back, "MM": middle_back, "IN": input_gradient, "GQ": collect,
+        "NB1": lambda: newton_back((5, 4, 3)), "NB2": lambda: newton_back((2, 1, 0)),
+    }
     for q in range(3):
-        gup_v[:, 256 * q : 256 * (q + 1)] = ups[q].finish()
-    stores.append(fetch(gup_v, gup_hbm))
-    total = outs.finish()
-    gout_v[:band_half] = total[:, :head_width]
-    gout_v[band_half:] = total[:, head_width:]
-    stores.append(fetch(gout_v, gout_hbm))
-    total = sum_step(4, pending)
-    ggain_v[...] = total[0:2]
-    gshift_v[...] = total[2:4]
-    gtaps_v[...] = total[4:16, :TAPS]
-    stores.append(fetch(ggain_v, ggain_hbm))
-    stores.append(fetch(gshift_v, gshift_hbm))
-    stores.append(fetch(gtaps_v, gtaps_hbm))
-    for index in range(3):
-        goal = quarters * index + me
-        source = lax.rem(3 * me + index, quarters)
-
-        @pl.when(lax.div(goal, 3) != me)
-        def _():
-            copy_to(fin.at[index], slots.at[0], sems, last + index, mate).wait_send()
-
-        @pl.when(source != me)
-        def _():
-            copy_to(fin.at[0], slots.at[index], sems, last + index, mate).wait_recv()
-
-    for index in range(3):
-        got = slots[index]
-        cols = slice(head_width * index, head_width * (index + 1))
-        gqkv_v[:band_half, cols] = got[:, :head_width]
-        gqkv_v[band_half:, cols] = got[:, head_width:]
-    stores.append(fetch(gqkv_v, gqkv_hbm))
+        table["UG%d" % q] = lambda q=q: up_gradient(q)
+        table["QG%d" % q] = lambda q=q: qkv_gradient(q)
+    for k in range(6):
+        table["S%d" % k] = lambda k=k: sum_step(k)
+    names = {"O": (outs, finish_out)}
+    for q in range(3):
+        names["D%d" % q] = (downs[q], lambda q=q: finish_down(q))
+        names["U%d" % q] = (ups[q], lambda q=q: finish_up(q))
+        names["P%d" % q] = (projs[q], lambda q=q: finish_proj(q))
+    for item in SCHEDULE:
+        if item in table:
+            table[item]()
+        else:
+            chunk, finish = names[item]
+            if chunk.stage == len(chunk.bits) - 1:
+                finish()
+            else:
+                chunk.step()
     for copy in stores:
         copy.wait()
 
@@ -756,7 +776,7 @@
         shape((band, w_qkv.shape[1] // 4), F32),
         shape((band, width // 4), F32),
         shape((band, ff // 4), F32),
-        shape((down_cols, width // 4), F32),
+        shape((width // 4, down_cols), F32),
         shape(norm_gains.shape, F32),
         shape(norm_shifts.shape, F32),
         shape(conv_kernels.shape, F32),
@@ -793,7 +813,7 @@
             VMEM((3 * head_width, slot), BF16),
             VMEM((3 * width, rows), BF16),
             VMEM((rows, width), F32), VMEM((rows, width), F32), VMEM((rows, width), F32),
-            VMEM((5, 16, width), F32), VMEM((5, 16, width), F32),
+            VMEM((5, 8, width), F32), VMEM((5, 8, width), F32),
             VMEM((3, band // 2, 2 * head_width), F32),
             VMEM((3, band // 2, 2 * head_width), F32),
             VMEM((3, 16, 64, down_cols), BF16), VMEM((3, 15, 64, down_cols), BF16),
@@ -812,7 +832,7 @@
         tokens, out_grad, w_qkv, w_out, w_up, w_down, norm_gains, norm_shifts, conv_kernels,
         seq_lengths, seg_bounds,
     )
-    return pl.pallas_call(
+    copied = pl.pallas_call(
         final_kernel,
         out_shape=outs,
         in_specs=[anywhere] * 9,
@@ -821,6 +841,8 @@
         + [pltpu.SemaphoreType.DMA((2, 9))],
         name="final_kernel",
     )(*found)
+    copied = tuple(copied)
+    return copied[:5] + (copied[5].T,) + copied[6:]
 
 
 highest = lax.Precision.HIGHEST

time: 114 us -> 107 us (0.939)
  Pallas kernels: 111 us -> 105 us
  local copies, waits for them, and re-layouts: 1.86 us -> 0 us
    pallas_call x1, Pallas kernels: 108 us -> 103 us  [per_device_fast(): pl.pallas_call(main_kernel, out_shape=outs, in_specs=[anywhere] * 6 + [wh...]
    pallas_call x1 -> x0, local copies, waits for them, and re-layouts: 1.86 us -> none  [per_device_fast(): pl.pallas_call(final_kernel, out_shape=outs, in_specs=[anywhere] * 9, out...]
where the time goes in v3:
time: 107 us; the launch traced here: 106 us
  Pallas kernels  105 us (98%)
  between operations  1.48 us (1%)
    pallas_call x1, Pallas kernels, per_device_fast(): pl.pallas_call(main_kernel, out_shape=outs, in_specs=[anywhere] * 6 + [wh...  103 us
    pallas_call x1, Pallas kernels, per_device_fast(): pl.pallas_call(final_kernel, out_shape=outs, in_specs=[anywhere] * 9, out...  2.35 us

profile of v3, /device:TPU:0, one launch (start us, length us, event | category | flops | bytes accessed | tf_op | source)
XLA Modules:
  0.0 106.4 jit_solution(434639784883200906)
XLA Ops:
  1.3 102.5 %main_kernel.1 = (bf16[256,768]{1,0:T(8,128)(2,1)}, bf16[256,768]{1,0:T(8,128)(2,1)}, f32[96,576]{1,0:T(8,128)}, f32[96,192]{1,0:T(8,128)}, f32[96,768]{1,0:T(8,...) custom-call(bf16[256,768]{1,0:T(8,128)(2,1)} %tok_hbm.1, ...), custom_call_target="tpu_custom_call" | custom-call | tf_op jit(solution)/shard_map/main_kernel/pallas_call | solution.py:784
  103.8 2.4 %final_kernel.1 = (bf16[256,768]{1,0:T(8,128)(2,1)}, bf16[256,768]{1,0:T(8,128)(2,1)}, f32[96,576]{1,0:T(8,128)}, f32[96,192]{1,0:T(8,128)}, f32[96,768]{1,0:T(8...) custom-call(bf16[256,768]{1,0:T(8,128)(2,1)} %get-tuple-element.27.refs_0_, ...), custom_call_target="tpu_custom_call" | custom-call | tf_op jit(solution)/shard_map/final_kernel/pallas_call | solution.py:835

commit v4 on v3

--- a/solution.py
+++ b/solution.py
@@ -190,16 +190,16 @@
     return spot
 
 
-DOWN_ORDERS = ("lyxh", "yxlh", "xlyh")
-UP_ORDERS = ("ylxh", "xylh", "xylh")
-OUT_ORDER = "lyhx"
-SUM_ORDER = "chlxy"
+DOWN_ORDERS = ("lyxh", "lxyh", "yxlh")
+UP_ORDERS = ("lyh", "ylh", "ylh")
+OUT_ORDER = "xylh"
+SUM_ORDER = "hlxyc"
 QKV_ORDERS = ("ylh", "ylh", "ylh")
 SCHEDULE = (
-    "DG", "FB", "UG0", "OG", "D0", "D1", "D2", "AV", "S0", "O", "QG2", "S1", "NB1", "U0",
-    "D1", "UG1", "NB2", "D2", "UG2", "SM", "S2", "D0", "MM", "O", "QG0", "U0", "QG1", "D1",
-    "P2", "S3", "D2", "U1", "O", "P0", "D1", "P2", "P1", "D2", "U2", "P0", "U1", "P2", "D0",
-    "P1", "P0", "U2", "U1", "D0", "IN", "P1", "U0", "U2", "S4", "O", "U1", "S5", "U0", "U2",
+    "DG", "LF", "FB", "D0", "D2", "GF", "UH", "UG0", "OG", "UG1", "D0", "AV", "S0", "D1",
+    "D2", "NB1", "SM", "U0", "S1", "U1", "QG2", "NB2", "D2", "O", "MM", "D0", "S2", "U1",
+    "U0", "QG0", "QG1", "D2", "UG2", "P2", "D0", "O", "U1", "D1", "U0", "P0", "P2", "O", "P1",
+    "P0", "P2", "IN", "U2", "S3", "O", "P1", "D1", "P0", "S4", "U2", "S5", "P1", "D1", "U2",
     "GQ",
 )
 
@@ -210,7 +210,7 @@
     out_hbm, in_hbm, gqkv_hbm, gout_hbm, gup_hbm, gdown_hbm, ggain_hbm, gshift_hbm, gtaps_hbm,
     tok, grad_in, w_qkv, w_out, w_up, w_down, lsem, sems,
     everyone, wt, bases, packed, a1, a3, chain, marks, att, heads, heads_x,
-    low_t, low_x, act, gst, gst_x, slope, gh, gh_x, gb, gb_x, gatt, g_in, gproj, gp_in,
+    low_all, g2_all, act, gst, gst_x, slope, gh, gb, gb_x, gatt, g_in, gproj, gp_in,
     first_ref, norm1_ref, gr1_ref, sum_s, sum_r, fin, slots,
     acc_down, got_down, acc_up, got_up, acc_out, got_out, acc_qkv, got_qkv,
     out_v, in_v, gqkv_v, gout_v, gup_v, gdown_v, ggain_v, gshift_v, gtaps_v,
@@ -387,8 +387,9 @@
     first_norm = normed * gain_ref[0:1] + shift_ref[0:1]
     first_ref[...] = first_norm
     low = first_norm.astype(BF16)
-    low_t[...] = low.T
-    low_sent = send(low_t, low_x, mate)
+    low_all[me] = low
+    low_far = send(low_all.at[me], low_all.at[me], (dp, me ^ 2))
+    low_near = send(low_all.at[me], low_all.at[me], mate)
     wup_fetch.wait()
     wdown_fetch.wait()
     second_sum = None
@@ -414,6 +415,9 @@
     g_two = norm_backward(cotangent, gain_ref[1:2], normed_two, root_two)
     gr1_ref[...] = g_two
     g_low = g_two.astype(BF16)
+    g2_all[me] = g_low
+    g2_far = send(g2_all.at[me], g2_all.at[me], (dp, me ^ 2))
+    g2_near = send(g2_all.at[me], g2_all.at[me], mate)
     gst[...] = g_low.T
     gst_sent = send(gst, gst_x, mate)
     for copy in act_sent:
@@ -455,15 +459,10 @@
 
     def forward_back():
         g_first = gr1_ref[...]
-        s["gh"] = []
         for i in range(quarters):
             cols = slice(block * i, block * (i + 1))
             part = (slope[:, cols] * mm(g_low, w_down[cols, :], 1, 1)).astype(BF16)
-            gh[:, cols] = part
             g_first = g_first + mm(part, w_up[:, cols], 1, 1)
-            if i % 2:
-                lanes = pl.ds(pl.multiple_of(block * (i - core), 128), block)
-                s["gh"].append(send(gh.at[:, lanes], gh_x.at[i // 2], mate))
         normed = norm1_ref[...]
         sum_s[0, 0:1] = jnp.sum(g_first * normed, axis=0, keepdims=True)
         sum_s[0, 2:3] = jnp.sum(g_first, axis=0, keepdims=True)
@@ -479,20 +478,39 @@
         s["gb"] = send(gb, gb_x, mate)
         g_in[:, mine] = gatt[own_rows]
 
+    own_cols = pl.ds(pl.multiple_of(block * me, 128), block)
+
+    def low_onward():
+        low_far.wait()
+        s["low"] = send(low_all.at[me ^ 2], low_all.at[me ^ 2], mate)
+
+    def g2_onward():
+        g2_far.wait()
+        s["g2"] = send(g2_all.at[me ^ 2], g2_all.at[me ^ 2], mate)
+
+    def up_slopes():
+        low_near.wait()
+        s["low"].wait()
+        side = w_up[:, own_cols]
+        for b in range(quarters):
+            hidden = mm(low_all[b], side, 1, 0)
+            slope[:, block * b : block * (b + 1)] = gelu_pair(hidden)[1]
+        s["low_t"] = low_all[...].reshape(slot, width).T
+
     def up_gradient(q):
         if q == 0:
-            low_sent.wait()
-            for copy in s["gh"]:
-                copy.wait()
-            s["lead"] = cat([low_t[...], low_x[...]], 1)
-        for x in range(2):
-            lanes = pl.ds(pl.multiple_of(block * (2 * x + core) + 256 * q, 128), 256)
-            side = cat([gh[:, lanes], gh_x[x, :, 256 * q : 256 * (q + 1)]], 0)
-            total = mm(s["lead"], side, 1, 0).astype(BF16)
-            for d in range(8):
-                acc_up[q, position(UP_ORDERS[q], places(x, d))] = total[
-                    band_rows * d : band_rows * (d + 1)
-                ]
+            g2_near.wait()
+            s["g2"].wait()
+            side = w_down[own_cols, :]
+            for b in range(quarters):
+                cols = slice(block * b, block * (b + 1))
+                gh[:, cols] = (slope[:, cols] * mm(g2_all[b], side, 1, 1)).astype(BF16)
+        side = cat([gh[:, block * b + 256 * q : block * b + 256 * (q + 1)] for b in range(4)], 0)
+        total = mm(s["low_t"], side, 1, 0).astype(BF16)
+        for d in range(8):
+            acc_up[q, position(UP_ORDERS[q], places(0, d))] = total[
+                band_rows * d : band_rows * (d + 1)
+            ]
         ups[q].start()
 
     def out_gradient():
@@ -714,6 +732,7 @@
     table = {
         "DG": down_gradient, "FB": forward_back, "OG": out_gradient, "AV": values_back,
         "SM": softmax_back, "MM": middle_back, "IN": input_gradient, "GQ": collect,
+        "LF": low_onward, "GF": g2_onward, "UH": up_slopes,
         "NB1": lambda: newton_back((5, 4, 3)), "NB2": lambda: newton_back((2, 1, 0)),
     }
     for q in range(3):
@@ -802,11 +821,11 @@
             VMEM((6, DIM, head_width), F32),
             VMEM((head_width, slot), BF16),
             VMEM((width, rows), BF16), VMEM((width, rows), BF16),
-            VMEM((width, rows), BF16), VMEM((width, rows), BF16),
+            VMEM((4, rows, width), BF16), VMEM((4, rows, width), BF16),
             VMEM((2 * rows, ff), BF16),
             VMEM((width, rows), BF16), VMEM((width, rows), BF16),
             VMEM((rows, ff), F32),
-            VMEM((rows, ff), BF16), VMEM((2, rows, ff // 4), BF16),
+            VMEM((rows, ff), BF16),
             VMEM((rows, width), BF16), VMEM((rows, width), BF16),
             VMEM((width, rows), BF16),
             VMEM((head_width, slot), BF16),
@@ -817,7 +836,7 @@
             VMEM((3, band // 2, 2 * head_width), F32),
             VMEM((3, band // 2, 2 * head_width), F32),
             VMEM((3, 16, 64, down_cols), BF16), VMEM((3, 15, 64, down_cols), BF16),
-            VMEM((3, 16, band, 256), BF16), VMEM((3, 15, band, 256), BF16),
+            VMEM((3, 8, band, 256), BF16), VMEM((3, 7, band, 256), BF16),
             VMEM((16, band // 2, 2 * head_width), BF16),
             VMEM((15, band // 2, 2 * head_width), BF16),
             VMEM((3, 8, band // 2, 2 * head_width), BF16),

time: 107 us -> 102 us (0.953)
  Pallas kernels: 105 us -> 100 us
    pallas_call x1, Pallas kernels: 103 us -> 97.8 us  [per_device_fast(): pl.pallas_call(main_kernel, out_shape=outs, in_specs=[anywhere] * 6 + [wh...]
where the time goes in v4:
time: 102 us
  Pallas kernels  100 us (98%)
  between operations  1.48 us (1%)
    pallas_call x1, Pallas kernels, per_device_fast(): pl.pallas_call(main_kernel, out_shape=outs, in_specs=[anywhere] * 6 + [wh...  97.8 us
    pallas_call x1, Pallas kernels, per_device_fast(): pl.pallas_call(final_kernel, out_shape=outs, in_specs=[anywhere] * 9, out...  2.35 us

profile of v4, /device:TPU:0, one launch (start us, length us, event | category | flops | bytes accessed | tf_op | source)
XLA Modules:
  0.0 101.7 jit_solution(441021029055228652)
XLA Ops:
  1.3 97.8 %main_kernel.1 = (bf16[256,768]{1,0:T(8,128)(2,1)}, bf16[256,768]{1,0:T(8,128)(2,1)}, f32[96,576]{1,0:T(8,128)}, f32[96,192]{1,0:T(8,128)}, f32[96,768]{1,0:T(8,...) custom-call(bf16[256,768]{1,0:T(8,128)(2,1)} %tok_hbm.1, ...), custom_call_target="tpu_custom_call" | custom-call | tf_op jit(solution)/shard_map/main_kernel/pallas_call | solution.py:803
  99.1 2.4 %final_kernel.1 = (bf16[256,768]{1,0:T(8,128)(2,1)}, bf16[256,768]{1,0:T(8,128)(2,1)}, f32[96,576]{1,0:T(8,128)}, f32[96,192]{1,0:T(8,128)}, f32[96,768]{1,0:T(8...) custom-call(bf16[256,768]{1,0:T(8,128)(2,1)} %get-tuple-element.27.refs_0_, ...), custom_call_target="tpu_custom_call" | custom-call | tf_op jit(solution)/shard_map/final_kernel/pallas_call | solution.py:854

commit v5 on v4

--- a/solution.py
+++ b/solution.py
@@ -136,7 +136,7 @@
     barrier = pltpu.get_barrier_semaphore()
     for device in devices:
         pl.semaphore_signal(barrier, inc=1, device_id=device, device_id_type=MESH)
-    pl.semaphore_wait(barrier, len(devices))
+    return lambda: pl.semaphore_wait(barrier, len(devices))
 
 
 class Spread:
@@ -190,17 +190,17 @@
     return spot
 
 
-DOWN_ORDERS = ("lyxh", "lxyh", "yxlh")
+DOWN_ORDERS = ("yxlh", "lyxh", "lxyh")
 UP_ORDERS = ("lyh", "ylh", "ylh")
-OUT_ORDER = "xylh"
-SUM_ORDER = "hlxyc"
+OUT_ORDER = "yxlh"
+SUM_ORDER = "hycxl"
 QKV_ORDERS = ("ylh", "ylh", "ylh")
 SCHEDULE = (
-    "DG", "LF", "FB", "D0", "D2", "GF", "UH", "UG0", "OG", "UG1", "D0", "AV", "S0", "D1",
-    "D2", "NB1", "SM", "U0", "S1", "U1", "QG2", "NB2", "D2", "O", "MM", "D0", "S2", "U1",
-    "U0", "QG0", "QG1", "D2", "UG2", "P2", "D0", "O", "U1", "D1", "U0", "P0", "P2", "O", "P1",
-    "P0", "P2", "IN", "U2", "S3", "O", "P1", "D1", "P0", "S4", "U2", "S5", "P1", "D1", "U2",
-    "GQ",
+    "HB0", "DG", "LF", "HB1", "FB", "OG", "D1", "D0", "GF", "UH", "UG0", "UG1", "O", "AV",
+    "S0", "D2", "D0", "SM", "D1", "NB1", "O", "U0", "S1", "QG2", "U1", "NB2", "D0", "MM", "O",
+    "U0", "QG0", "S2", "U1", "QG1", "UG2", "S3", "D2", "D0", "P2", "D1", "O", "P0", "U0",
+    "U1", "P1", "P2", "D1", "IN", "S4", "U2", "P0", "P1", "D2", "P2", "S5", "U2", "P0", "P1",
+    "D2", "U2", "GQ",
 )
 
 
@@ -257,10 +257,11 @@
     def spread(acc, got, order):
         return Spread(acc, got, [bits[name] for name in order], sems, reserve(len(order)))
 
+    all_here = greet([(dp, me ^ k) for k in (1, 2, 3)] + [(dp ^ k, me) for k in (1, 2, 4)])
     own_fetch = fetch(tok_hbm, everyone.at[me])
     tok_fetch = fetch(tok_hbm, tok)
     wqkv_fetch = fetch(wqkv_hbm, w_qkv)
-    greet([(dp, me ^ k) for k in (1, 2, 3)] + [(dp ^ k, me) for k in (1, 2, 4)])
+    all_here()
     half = rows // 2
     far = []
     for piece in range(2):
@@ -365,16 +366,17 @@
     f_high, f_low = halves(first)
     mixed = mm(cat([packs.block(w_high), packs.block(w_low)], 0), f_high, 1, 0)
     mixed = mixed[:head_width] + mixed[head_width:] + mm(packs.block(w_high), f_low, 1, 0)
+    mine = pl.ds(pl.multiple_of(rows * me, rows), rows)
+    own_rows = pl.ds(pl.multiple_of(head_width * me, 64), head_width)
+    att_sent = []
     for h in range(nh):
         part = slice(DIM * h, DIM * (h + 1))
         conv = unwindow(mm(windows(values[part]), bands[0][h], 1, 1), DIM)
         att[part] = jnp.where(live, mixed[part] + conv, 0.0).astype(BF16)
-    mine = pl.ds(pl.multiple_of(rows * me, rows), rows)
-    own_rows = pl.ds(pl.multiple_of(head_width * me, 64), head_width)
-    att_sent = []
-    for k in (2, 3, 1):
-        lanes = pl.ds(pl.multiple_of(rows * (me ^ k), rows), rows)
-        att_sent.append(send(att.at[:, lanes], heads.at[own_rows], (dp, me ^ k)))
+        goal = pl.ds(pl.multiple_of(head_width * me + DIM * h, 64), DIM)
+        for k in (2, 3, 1):
+            lanes = pl.ds(pl.multiple_of(rows * (me ^ k), rows), rows)
+            att_sent.append(send(att.at[part, lanes], heads.at[goal], (dp, me ^ k)))
     heads[own_rows] = att[:, mine]
     wout_fetch.wait()
     tok_fetch.wait()
@@ -404,25 +406,22 @@
         part = mm(active, w_down[cols, :], 1, 0)
         second_sum = part if second_sum is None else second_sum + part
     normed_two, root_two = norm_forward(first_ref[...] + second_sum)
-    out_v[...] = (normed_two * gain_ref[1:2] + shift_ref[1:2]).astype(BF16)
-    stores = [fetch(out_v, out_hbm)]
     grad_fetch.wait()
     spot = me * rows + lax.broadcasted_iota(jnp.int32, (rows, 1), 0)
     cotangent = jnp.where(spot < length, grad_in[...].astype(F32), 0.0)
+    g_two = norm_backward(cotangent, gain_ref[1:2], normed_two, root_two)
+    g_low = g_two.astype(BF16)
+    g2_all[me] = g_low
+    g2_far = send(g2_all.at[me], g2_all.at[me], (dp, me ^ 2))
+    gst[...] = g_low.T
+    gst_sent = send(gst, gst_x, mate)
+    g2_near = send(g2_all.at[me], g2_all.at[me], mate)
+    gr1_ref[...] = g_two
+    out_v[...] = (normed_two * gain_ref[1:2] + shift_ref[1:2]).astype(BF16)
+    stores = [fetch(out_v, out_hbm)]
     sum_s[0] = jnp.zeros(sum_s.shape[1:], F32)
     sum_s[0, 1:2] = jnp.sum(cotangent * normed_two, axis=0, keepdims=True)
     sum_s[0, 3:4] = jnp.sum(cotangent, axis=0, keepdims=True)
-    g_two = norm_backward(cotangent, gain_ref[1:2], normed_two, root_two)
-    gr1_ref[...] = g_two
-    g_low = g_two.astype(BF16)
-    g2_all[me] = g_low
-    g2_far = send(g2_all.at[me], g2_all.at[me], (dp, me ^ 2))
-    g2_near = send(g2_all.at[me], g2_all.at[me], mate)
-    gst[...] = g_low.T
-    gst_sent = send(gst, gst_x, mate)
-    for copy in act_sent:
-        copy.wait()
-    gst_sent.wait()
     s = {}
     downs = [spread(acc_down.at[q], got_down.at[q], DOWN_ORDERS[q]) for q in range(3)]
     ups = [spread(acc_up.at[q], got_up.at[q], UP_ORDERS[q]) for q in range(3)]
@@ -441,6 +440,9 @@
         return {"x": x, "y": d % 2, "l": d // 2 % 2, "h": d // 4}
 
     def down_gradient():
+        for copy in act_sent:
+            copy.wait()
+        gst_sent.wait()
         tops = [pl.ds(pl.multiple_of(head_width * (2 * x + core), 64), head_width) for x in (0, 1)]
         lead = cat([cat([gst[top, :], gst_x[top, :]], 1) for top in tops], 0)
         for pair in range(4):
@@ -457,12 +459,16 @@
         for chunk in downs:
             chunk.start()
 
-    def forward_back():
-        g_first = gr1_ref[...]
-        for i in range(quarters):
+    def hidden_back(turns):
+        g_first = s.get("g_first", g_two)
+        for i in turns:
             cols = slice(block * i, block * (i + 1))
             part = (slope[:, cols] * mm(g_low, w_down[cols, :], 1, 1)).astype(BF16)
             g_first = g_first + mm(part, w_up[:, cols], 1, 1)
+        s["g_first"] = g_first
+
+    def branch_back():
+        g_first = s["g_first"]
         normed = norm1_ref[...]
         sum_s[0, 0:1] = jnp.sum(g_first * normed, axis=0, keepdims=True)
         sum_s[0, 2:3] = jnp.sum(g_first, axis=0, keepdims=True)
@@ -730,7 +736,10 @@
         stores.append(fetch(gqkv_v, gqkv_hbm))
 
     table = {
-        "DG": down_gradient, "FB": forward_back, "OG": out_gradient, "AV": values_back,
+        "DG": down_gradient, "FB": branch_back,
+        "HB0": lambda: hidden_back((0,)), "HB1": lambda: hidden_back((1, 2, 3)),
+        "HB2": lambda: hidden_back((0, 1)), "HB3": lambda: hidden_back((2, 3)),
+        "OG": out_gradient, "AV": values_back,
         "SM": softmax_back, "MM": middle_back, "IN": input_gradient, "GQ": collect,
         "LF": low_onward, "GF": g2_onward, "UH": up_slopes,
         "NB1": lambda: newton_back((5, 4, 3)), "NB2": lambda: newton_back((2, 1, 0)),

time: 102 us -> 99.7 us (0.977)
  Pallas kernels: 100 us -> 98 us
    pallas_call x1, Pallas kernels: 97.8 us -> 95.7 us  [per_device_fast(): pl.pallas_call(main_kernel, out_shape=outs, in_specs=[anywhere] * 6 + [wh...]
where the time goes in v5:
time: 99.7 us; the launch traced here: 99.5 us
  Pallas kernels  98 us (98%)
  between operations  1.48 us (1%)
    pallas_call x1, Pallas kernels, per_device_fast(): pl.pallas_call(main_kernel, out_shape=outs, in_specs=[anywhere] * 6 + [wh...  95.7 us
    pallas_call x1, Pallas kernels, per_device_fast(): pl.pallas_call(final_kernel, out_shape=outs, in_specs=[anywhere] * 9, out...  2.35 us

profile of v5, /device:TPU:0, one launch (start us, length us, event | category | flops | bytes accessed | tf_op | source)
XLA Modules:
  0.0 99.5 jit_solution(15394297100248233456)
XLA Ops:
  1.3 95.7 %main_kernel.1 = (bf16[256,768]{1,0:T(8,128)(2,1)}, bf16[256,768]{1,0:T(8,128)(2,1)}, f32[96,576]{1,0:T(8,128)}, f32[96,192]{1,0:T(8,128)}, f32[96,768]{1,0:T(8,...) custom-call(bf16[256,768]{1,0:T(8,128)(2,1)} %tok_hbm.1, ...), custom_call_target="tpu_custom_call" | custom-call | tf_op jit(solution)/shard_map/main_kernel/pallas_call | solution.py:812
  97.0 2.4 %final_kernel.1 = (bf16[256,768]{1,0:T(8,128)(2,1)}, bf16[256,768]{1,0:T(8,128)(2,1)}, f32[96,576]{1,0:T(8,128)}, f32[96,192]{1,0:T(8,128)}, f32[96,768]{1,0:T(8...) custom-call(bf16[256,768]{1,0:T(8,128)(2,1)} %get-tuple-element.27.refs_0_, ...), custom_call_target="tpu_custom_call" | custom-call | tf_op jit(solution)/shard_map/final_kernel/pallas_call | solution.py:863

commit v6 on v5

--- a/solution.py
+++ b/solution.py
@@ -190,17 +190,17 @@
     return spot
 
 
-DOWN_ORDERS = ("yxlh", "lyxh", "lxyh")
+DOWN_ORDERS = ("lxyh", "lxyh", "yxlh")
 UP_ORDERS = ("lyh", "ylh", "ylh")
-OUT_ORDER = "yxlh"
-SUM_ORDER = "hycxl"
+OUT_ORDER = "xylh"
+SUM_ORDER = "lhcyx"
 QKV_ORDERS = ("ylh", "ylh", "ylh")
 SCHEDULE = (
-    "HB0", "DG", "LF", "HB1", "FB", "OG", "D1", "D0", "GF", "UH", "UG0", "UG1", "O", "AV",
-    "S0", "D2", "D0", "SM", "D1", "NB1", "O", "U0", "S1", "QG2", "U1", "NB2", "D0", "MM", "O",
-    "U0", "QG0", "S2", "U1", "QG1", "UG2", "S3", "D2", "D0", "P2", "D1", "O", "P0", "U0",
-    "U1", "P1", "P2", "D1", "IN", "S4", "U2", "P0", "P1", "D2", "P2", "S5", "U2", "P0", "P1",
-    "D2", "U2", "GQ",
+    "HB0", "DG", "HB1", "FB", "UH0", "LF", "UGA", "D2", "D0", "GF", "OG", "UH1", "UGB", "UG0",
+    "UG1", "AV", "S0", "QG2", "D1", "NB1", "D2", "UG2", "SN", "U1", "SM", "U0", "D0", "S1",
+    "NB2", "P2", "D2", "MM", "U1", "QG0", "S2", "QG1", "U2", "O", "P2", "S3", "D2", "U0",
+    "U1", "D0", "U2", "P2", "P0", "U0", "D1", "D0", "P1", "U2", "P0", "O", "S4", "P1", "P0",
+    "D1", "IN", "P1", "O", "S5", "D1", "O", "GQ",
 )
 
 
@@ -262,9 +262,9 @@
     tok_fetch = fetch(tok_hbm, tok)
     wqkv_fetch = fetch(wqkv_hbm, w_qkv)
     all_here()
-    half = rows // 2
+    half = rows // 4
     far = []
-    for piece in range(2):
+    for piece in range(4):
         part = pl.ds(piece * half, half)
         far.append(send(tok_hbm.at[part], everyone.at[me, part], (dp, me ^ 2)))
     near = send(tok_hbm, everyone.at[me], mate)
@@ -307,7 +307,7 @@
     near.wait()
     project(me ^ 1)
     onward = []
-    for piece in range(2):
+    for piece in range(4):
         part = pl.ds(piece * half, half)
         far[piece].wait()
         onward.append(send(everyone.at[me ^ 2, part], everyone.at[me ^ 2, part], mate))
@@ -464,6 +464,7 @@
         for i in turns:
             cols = slice(block * i, block * (i + 1))
             part = (slope[:, cols] * mm(g_low, w_down[cols, :], 1, 1)).astype(BF16)
+            gh[:, cols] = part
             g_first = g_first + mm(part, w_up[:, cols], 1, 1)
         s["g_first"] = g_first
 
@@ -494,23 +495,33 @@
         g2_far.wait()
         s["g2"] = send(g2_all.at[me ^ 2], g2_all.at[me ^ 2], mate)
 
-    def up_slopes():
-        low_near.wait()
-        s["low"].wait()
+    def block_cols(b):
+        return pl.ds(pl.multiple_of(block * b, 128), block)
+
+    def up_slopes(turns):
         side = w_up[:, own_cols]
-        for b in range(quarters):
-            hidden = mm(low_all[b], side, 1, 0)
-            slope[:, block * b : block * (b + 1)] = gelu_pair(hidden)[1]
-        s["low_t"] = low_all[...].reshape(slot, width).T
+        for turn in turns:
+            if turn == 1:
+                low_near.wait()
+            if turn == 3:
+                s["low"].wait()
+            hidden = mm(low_all[me ^ turn], side, 1, 0)
+            slope[:, block_cols(me ^ turn)] = gelu_pair(hidden)[1]
+        if 3 in turns:
+            s["low_t"] = low_all[...].reshape(slot, width).T
+
+    def up_hidden(turns):
+        side = w_down[own_cols, :]
+        for turn in turns:
+            if turn == 1:
+                g2_near.wait()
+            if turn == 3:
+                s["g2"].wait()
+            cols = block_cols(me ^ turn)
+            back = mm(g2_all[me ^ turn], side, 1, 1)
+            gh[:, cols] = (slope[:, cols] * back).astype(BF16)
 
     def up_gradient(q):
-        if q == 0:
-            g2_near.wait()
-            s["g2"].wait()
-            side = w_down[own_cols, :]
-            for b in range(quarters):
-                cols = slice(block * b, block * (b + 1))
-                gh[:, cols] = (slope[:, cols] * mm(g2_all[b], side, 1, 1)).astype(BF16)
         side = cat([gh[:, block * b + 256 * q : block * b + 256 * (q + 1)] for b in range(4)], 0)
         total = mm(s["low_t"], side, 1, 0).astype(BF16)
         for d in range(8):
@@ -621,25 +632,26 @@
             outer, hold = pair[:count], pair[count:] + 0.25 * rest
         s["outer"], s["hold"] = outer, hold
 
+    def tall_marks(high, low, wide):
+        both = mm(cat([high, low], 0), wide, 1, 1)
+        return packs.diagonal(both[:head_width] + both[head_width:]) * scale
+
     def softmax_back():
-        first, third = a1[...], a3[...]
+        first = a1[...]
         w_high, w_low = halves(marks[5])
         g_tall = mm(packs.block(w_high), s["grad"], 0, 0) + mm(packs.block(w_low), s["grad"], 0, 0)
         along = jnp.sum(per_head(g_tall * first), axis=1, keepdims=True)
         g_one = first * (per_head(g_tall) - along).reshape(head_width, slot)
+        s["one"], one_low = halves(g_one)
+        s["g_k"] = tall_marks(s["one"], one_low, packed[:head_width])
+
+    def places_back():
+        third = a3[...]
         g_tall = mm(cat([packs.block(s["s_high"]), packs.block(s["s_low"])], 0), s["values"], 1, 0)
         g_tall = g_tall[:head_width] + g_tall[head_width:]
         g_three = third * (g_tall - jnp.sum(g_tall * third, axis=1, keepdims=True))
-
-        def tall_marks(high, low, wide):
-            both = mm(cat([high, low], 0), wide, 1, 1)
-            return packs.diagonal(both[:head_width] + both[head_width:]) * scale
-
-        one_high, one_low = halves(g_one)
-        three_high, three_low = halves(g_three)
-        s["g_k"] = tall_marks(one_high, one_low, packed[:head_width])
-        s["g_q"] = tall_marks(three_high, three_low, packed[head_width : 2 * head_width])
-        s["one"], s["three"] = one_high, three_high
+        s["three"], three_low = halves(g_three)
+        s["g_q"] = tall_marks(s["three"], three_low, packed[head_width : 2 * head_width])
 
     def middle_back():
         q_marks, k_marks, middle = marks[0], marks[1], marks[2]
@@ -741,7 +753,10 @@
         "HB2": lambda: hidden_back((0, 1)), "HB3": lambda: hidden_back((2, 3)),
         "OG": out_gradient, "AV": values_back,
         "SM": softmax_back, "MM": middle_back, "IN": input_gradient, "GQ": collect,
-        "LF": low_onward, "GF": g2_onward, "UH": up_slopes,
+        "LF": low_onward, "GF": g2_onward,
+        "UH0": lambda: up_slopes((1,)), "UH1": lambda: up_slopes((2, 3)),
+        "UGA": lambda: up_hidden((1,)), "UGB": lambda: up_hidden((2, 3)),
+        "SN": places_back,
         "NB1": lambda: newton_back((5, 4, 3)), "NB2": lambda: newton_back((2, 1, 0)),
     }
     for q in range(3):

time: 99.7 us -> 99.3 us (level)
  no operation moved by 1% of the time
where the time goes in v6:
time: 99.3 us; the launch traced here: 99.1 us
  Pallas kernels  97.6 us (98%)
  between operations  1.48 us (1%)
    pallas_call x1, Pallas kernels, per_device_fast(): pl.pallas_call(main_kernel, out_shape=outs, in_specs=[anywhere] * 6 + [wh...  95.2 us
    pallas_call x1, Pallas kernels, per_device_fast(): pl.pallas_call(final_kernel, out_shape=outs, in_specs=[anywhere] * 9, out...  2.35 us

profile of v6, /device:TPU:0, one launch (start us, length us, event | category | flops | bytes accessed | tf_op | source)
XLA Modules:
  0.0 99.1 jit_solution(7378368440217594125)
XLA Ops:
  1.3 95.2 %main_kernel.1 = (bf16[256,768]{1,0:T(8,128)(2,1)}, bf16[256,768]{1,0:T(8,128)(2,1)}, f32[96,576]{1,0:T(8,128)}, f32[96,192]{1,0:T(8,128)}, f32[96,768]{1,0:T(8,...) custom-call(bf16[256,768]{1,0:T(8,128)(2,1)} %tok_hbm.1, ...), custom_call_target="tpu_custom_call" | custom-call | tf_op jit(solution)/shard_map/main_kernel/pallas_call | solution.py:827
  96.5 2.4 %final_kernel.1 = (bf16[256,768]{1,0:T(8,128)(2,1)}, bf16[256,768]{1,0:T(8,128)(2,1)}, f32[96,576]{1,0:T(8,128)}, f32[96,192]{1,0:T(8,128)}, f32[96,768]{1,0:T(8...) custom-call(bf16[256,768]{1,0:T(8,128)(2,1)} %get-tuple-element.27.refs_0_, ...), custom_call_target="tpu_custom_call" | custom-call | tf_op jit(solution)/shard_map/final_kernel/pallas_call | solution.py:878
